TPU v7x, 32 devices: a whole 2x2x4 slice. The times are simulated.
32 devices in a mesh: section: 8 (over z, y), dp: 2 (over x), mp: 2 (over core).
Axes of the slice: x: 2, y: 2, z: 4, core: 2. Of those that a mesh axis runs over, the one named last changes fastest.
Arguments:
- old_w: float32 [8, 2, 8, 208, 3328], P(None, 'dp', 'section', None, 'mp'), may hold values from -0.109375 to 0.109375
- old_m: bfloat16 [8, 2, 8, 208, 3328], P(None, 'dp', 'section', None, 'mp'), may hold values from -12 to 12
- old_v: bfloat16 [8, 2, 8, 208, 3328], P(None, 'dp', 'section', None, 'mp'), may hold values from 0.5 to 20
- old_slot_layer: int32 [8], replicated, may hold values from 0 to 7, each once
- norm_gain: float32 [8, 3328], P('section'), may hold values from 0.5 to 2
- tokens: bfloat16 [8, 32, 3328], P(None, 'dp'), may hold values from -6 to 6
- cotangent: bfloat16 [8, 32, 3328], P(None, 'dp'), may hold values from -6 to 6
Outputs:
- new_w: float32 [8, 3328, 3328], P('section', 'dp', 'mp')
- new_m: bfloat16 [8, 3328, 3328], P('section', 'dp', 'mp')
- new_v: bfloat16 [8, 3328, 3328], P('section', 'dp', 'mp')
Inputs may be any that keep to these rules, and one draw needn't show every extreme that they name: `old_slot_layer`: every layer number appears exactly once.
All inputs are finite; a program needn't handle non-finite values.
Results may differ from a plain program's by a relative error of at most 0.028.
Values may be sent and summed in bfloat16 or wider, within the bound.
No kernel may reach another device: no remote copies, remote signals or barrier semaphores. Data moves between devices by JAX's collectives and lax.ppermute only.
A program may use at most 128 MiB of HBM per device.

v0:
```python
import jax
import jax.numpy as jnp
from jax import lax
from jax.sharding import PartitionSpec as P

eps_norm = 1e-05
beta_one = 0.9
beta_two = 0.95
learn_rate = 0.001
decay_rate = 0.1
adam_eps = 1e-08
step_count = 1000.0


def from_behind(value, axis, by):
    count = lax.axis_size(axis)
    pairs = [(i, i + by) for i in range(count) if 0 <= i + by < count]
    return lax.ppermute(value, axis, pairs)


def silu_slope(values):
    sigmoid_value = jax.nn.sigmoid(values)
    return sigmoid_value * (1.0 + values * (1.0 - sigmoid_value))


def row_scale_of(inputs):
    widened = inputs.astype(jnp.float32)
    return lax.rsqrt(jnp.mean(widened * widened, axis=1, keepdims=True) + eps_norm)


def local(old_w, old_m, old_v, old_slot_layer, norm_gain, tokens, cotangent):
    sections = lax.axis_size("section")
    section_index = lax.axis_index("section")
    core_index = lax.axis_index("mp")
    micro_count = tokens.shape[0]
    row_count = tokens.shape[1]
    full_width = tokens.shape[2]
    piece_rows = old_w.shape[3]
    half_width = old_w.shape[4]
    row_block = sections * piece_rows
    token_total = micro_count * row_count
    ticks = micro_count + sections - 1
    layer_ids = jnp.arange(sections, dtype=jnp.int32)
    matches = (old_slot_layer[None, :] == layer_ids[:, None]).astype(jnp.int32)
    inverse = jnp.sum(matches * layer_ids[None, :], axis=1)
    ordered_w = jnp.take(old_w, inverse, axis=0)
    ordered_m = jnp.take(old_m, inverse, axis=0)
    ordered_v = jnp.take(old_v, inverse, axis=0)
    master = (
        lax.all_to_all(
            ordered_w.astype(jnp.bfloat16), "section", split_axis=0, concat_axis=2, tiled=True
        )
        .astype(ordered_w.dtype)
        .reshape(row_block, half_width)
    )
    moment_one, moment_two = (
        lax.all_to_all(ordered_m, "section", split_axis=0, concat_axis=2, tiled=True),
        lax.all_to_all(ordered_v, "section", split_axis=0, concat_axis=2, tiled=True),
    )
    moment_one = moment_one.reshape(row_block, half_width)
    moment_two = moment_two.reshape(row_block, half_width)
    weight_copy = lax.all_gather(master.astype(jnp.bfloat16), "dp", axis=0, tiled=True)
    gain_row = norm_gain[0]
    col_start = core_index * half_width
    gain_half = lax.dynamic_slice_in_dim(gain_row, col_start, half_width, 0)

    def layer_forward(inputs):
        row_scale = row_scale_of(inputs)
        normed = (inputs.astype(jnp.float32) * row_scale * gain_row).astype(jnp.bfloat16)
        preact = jnp.dot(normed, weight_copy, preferred_element_type=jnp.float32)
        own_cols = lax.dynamic_slice_in_dim(inputs, col_start, half_width, 1).astype(jnp.float32)
        return ((own_cols + jax.nn.silu(preact)).astype(jnp.bfloat16), normed, preact)

    def forward_send(output):
        moved = from_behind(output, "section", 1)
        return lax.all_gather(moved, "mp", axis=1, tiled=True)

    def forward_tick(tick_index, loop_carry):
        arriving, stashed, normed_cols, preacts = loop_carry
        batch_index = tick_index - section_index
        active = (batch_index >= 0) & (batch_index < micro_count)
        slot_index = jnp.clip(batch_index, 0, micro_count - 1)
        entry_rows = lax.dynamic_index_in_dim(tokens, slot_index, 0, keepdims=False)
        inputs = jnp.where(section_index == 0, entry_rows, arriving)

        def forward_do_work(stash_state):
            stash_acts, stash_normed, stash_pre = stash_state
            output, normed, preact = layer_forward(inputs)
            stash_acts = lax.dynamic_update_index_in_dim(stash_acts, inputs, slot_index, 0)
            stash_normed = lax.dynamic_update_slice_in_dim(
                stash_normed, normed.T, slot_index * row_count, 1
            )
            stash_pre = lax.dynamic_update_index_in_dim(stash_pre, preact, slot_index, 0)
            return (output, (stash_acts, stash_normed, stash_pre))

        def skip_work(stash_state):
            return (jnp.zeros((row_count, half_width), jnp.bfloat16), stash_state)

        output, stash_state = lax.cond(
            active, forward_do_work, skip_work, (stashed, normed_cols, preacts)
        )
        arriving = forward_send(output)
        return (arriving,) + stash_state

    forward_init = (
        jnp.zeros((row_count, full_width), jnp.bfloat16),
        jnp.zeros((micro_count, row_count, full_width), jnp.bfloat16),
        jnp.zeros((full_width, token_total), jnp.bfloat16),
        jnp.zeros((micro_count, row_count, half_width), jnp.float32),
    )
    _, stashed, normed_cols, preacts = lax.fori_loop(0, ticks, forward_tick, forward_init)

    def grad_part(own_grad, slot_index, dpre_rows):
        preact = lax.dynamic_index_in_dim(preacts, slot_index, 0, keepdims=False)
        dpre = (own_grad.astype(jnp.float32) * silu_slope(preact)).astype(jnp.bfloat16)
        partial_value = lax.dot_general(
            dpre, weight_copy, (((1,), (1,)), ((), ())), preferred_element_type=jnp.float32
        )
        dpre_rows = lax.dynamic_update_slice_in_dim(dpre_rows, dpre, slot_index * row_count, 0)
        return (partial_value, dpre_rows)

    def skip_part(dpre_rows):
        return (jnp.zeros((row_count, full_width), jnp.float32), dpre_rows)

    dpre_init = jnp.zeros((token_total, half_width), jnp.bfloat16)

    def backward_tick(tick_index, loop_carry):
        arriving, dpre_rows = loop_carry
        batch_index = tick_index - (sections - 1 - section_index)
        active = (batch_index >= 0) & (batch_index < micro_count)
        slot_index = jnp.clip(batch_index, 0, micro_count - 1)
        seed_grad = lax.dynamic_index_in_dim(cotangent, slot_index, 0, keepdims=False)
        seed_half = lax.dynamic_slice_in_dim(seed_grad, col_start, half_width, 1)
        upstream = jnp.where(section_index == sections - 1, seed_half, arriving)

        def backward_do_work(rows_state):
            return grad_part(upstream, slot_index, rows_state)

        partial_value, dpre_rows = lax.cond(active, backward_do_work, skip_part, dpre_rows)
        summed_half = lax.psum_scatter(
            partial_value.astype(jnp.bfloat16), "mp", scatter_dimension=1, tiled=True
        ).astype(jnp.float32)
        inputs = lax.dynamic_index_in_dim(stashed, slot_index, 0, keepdims=False)
        row_scale = row_scale_of(inputs)
        inputs_half = lax.dynamic_slice_in_dim(inputs, col_start, half_width, 1).astype(jnp.float32)
        weighted = gain_half * summed_half
        stat_part = jnp.sum(inputs_half * weighted, axis=1, keepdims=True)
        row_stat = lax.psum(stat_part, "mp") / full_width
        cube = row_scale * row_scale * row_scale
        back_half = (
            upstream.astype(jnp.float32) + row_scale * weighted - inputs_half * cube * row_stat
        ).astype(jnp.bfloat16)
        arriving = from_behind(back_half, "section", -1)
        return (arriving, dpre_rows)

    backward_init = (jnp.zeros((row_count, half_width), jnp.bfloat16), dpre_init)
    _, dpre_rows = lax.fori_loop(0, ticks, backward_tick, backward_init)
    features = lax.all_to_all(normed_cols, "dp", split_axis=0, concat_axis=1, tiled=True)
    weight_grad = jnp.dot(
        features,
        lax.all_gather(dpre_rows, "dp", axis=0, tiled=True),
        preferred_element_type=jnp.float32,
    )
    moment_next = beta_one * moment_one.astype(jnp.float32) + (1.0 - beta_one) * weight_grad
    second_next = (
        beta_two * moment_two.astype(jnp.float32) + (1.0 - beta_two) * weight_grad * weight_grad
    )
    fix_one = 1.0 - beta_one**step_count
    fix_two = 1.0 - beta_two**step_count
    direction = moment_next / fix_one / (jnp.sqrt(second_next / fix_two) + adam_eps)
    updated = master - learn_rate * (direction + decay_rate * master)
    return (
        updated[None],
        moment_next.astype(jnp.bfloat16)[None],
        second_next.astype(jnp.bfloat16)[None],
    )


def solution(mesh):
    placed = (
        P(None, "dp", "section", None, "mp"),
        P(None, "dp", "section", None, "mp"),
        P(None, "dp", "section", None, "mp"),
        P(),
        P("section", None),
        P(None, "dp", None),
        P(None, "dp", None),
    )
    return jax.shard_map(
        local,
        mesh=mesh,
        in_specs=placed,
        out_specs=(P("section", "dp", "mp"), P("section", "dp", "mp"), P("section", "dp", "mp")),
        check_vma=False,
    )
```

profile of v0, /device:TPU:0, one launch (start us, length us, event | category | flops | bytes accessed | tf_op | source)
XLA Modules:
  0.0 1118.9 jit_solution(13006870590378239135)
XLA Ops:
  20.3 7.7 gather_fusion
  28.0 12.0 %bitcast_select_fusion.3 = (bf16[8,1,1,208,1664]{4,3,2,1,0:T(8,128)(2,1)}, bf16[8,1,1,208,1664]{4,3,2,1,0:T(8,128)(2,1)}, bf16[8,1,1,208,1664]{4,3,2,1,0:T(8,128)(2,1)S(1)}) fusion(bf16[8,208,1664]{2,1,0:T(8,128)(2,1)} %gather_fusion.2, pred[8]{0:T(512)(128)(4,1)S(1)} %compare_and_fusion, bf16[8,208,1664]{2,1,0:T(8,128)(2,1)} %gather_fusion.1, ...), kind=kLoop, calls=%fused_computation.50 | loop fusion | flops 8306688 | bytes 33226760 | tf_op jit(solution)/shard_map/jit(_take)/select_n | solution.py:48
  40.0 129.9 %all_to_all.49 = bf16[8,1,1,208,1664]{4,3,2,1,0:T(8,128)(2,1)} all-to-all(bf16[8,1,1,208,1664]{4,3,2,1,0:T(8,128)(2,1)S(1)} %get-tuple-element.729), channel_id=1, replica_groups=mesh['section'=8,'dp'=2,'mp'=2] {'section'}, dimensions={0} | all-to-all | bytes 11075584 | tf_op jit(solution)/shard_map/all_to_all | solution.py:50
  175.4 120.5 %all-to-all-done.1 = bf16[8,1,1,208,1664]{4,3,2,1,0:T(8,128)(2,1)} async-done(((bf16[8,1,1,208,1664]{4,3,2,1,0:T(8,128)(2,1)}), bf16[8,1,1,208,1664]{4,3,2,1,0:T(8,128)(2,1)}, u32[]{:S(2)}, u32[]{:S(2)}) %all-to-all-start.1) | async-done | bytes 5537824 | tf_op jit(solution)/shard_map/all_to_all | solution.py:57
  300.7 7.6 convert_multiply_fusion.7
  308.3 113.6 %all-to-all-done.3 = bf16[8,1,1,208,1664]{4,3,2,1,0:T(8,128)(2,1)} async-done(((bf16[8,1,1,208,1664]{4,3,2,1,0:T(8,128)(2,1)}), bf16[8,1,1,208,1664]{4,3,2,1,0:T(8,128)(2,1)}, u32[]{:S(2)}, u32[]{:S(2)}) %all-to-all-start.3) | async-done | bytes 5537824 | tf_op jit(solution)/shard_map/all_to_all | solution.py:58
  421.8 7.6 convert_multiply_fusion.6
  429.6 201.0 %while.41 = (s32[]{:T(128)}, bf16[16,3328]{1,0:T(8,128)(2,1)S(1)}, bf16[8,16,3328]{2,1,0:T(8,128)(2,1)S(1)}, bf16[3328,128]{0,1:T(8,128)(2,1)S(1)}, f32[8,16,166...) while((s32[]{:T(128)}, bf16[16,3328]{1,0:T(8,128)(2,1)S(1)}, ...), condition=%wide.region_5.7_spmd, body=%wide.region_1.6_spmd.sunk | while | flops 178034704 | bytes 12787352 | solution.py:111
  548.2 12.1 %collective-permute-start = (bf16[16,1664]{1,0:T(8,128)(2,1)S(1)}, bf16[16,1664]{1,0:T(8,128)(2,1)S(1)}, u32[]{:S(2)}, u32[]{:S(2)}) collective-permute-start(bf16[16,1664]{1,0:T(8,128)(2,1)S(1)} %get-tuple-element.861), channel_id=1, source_target_pairs={{0,4},{4,8},{8,12},{12,16},{16,20},{20,24},{24,28},{1,5},{5,9},{9,... | collective-permute-start | bytes 159752 | tf_op jit(solution)/shard_map/while/body/eval_jaxpr/ppermute | solution.py:18
  572.9 12.1 %collective-permute-start = (bf16[16,1664]{1,0:T(8,128)(2,1)S(1)}, bf16[16,1664]{1,0:T(8,128)(2,1)S(1)}, u32[]{:S(2)}, u32[]{:S(2)}) collective-permute-start(bf16[16,1664]{1,0:T(8,128)(2,1)S(1)} %get-tuple-element.861), channel_id=1, source_target_pairs={{0,4},{4,8},{8,12},{12,16},{16,20},{20,24},{24,28},{1,5},{5,9},{9,... | collective-permute-start | bytes 159752 | tf_op jit(solution)/shard_map/while/body/eval_jaxpr/ppermute | solution.py:18
  597.5 8.1 collective-permute-start
  618.0 8.9 collective-permute-start
  635.5 446.4 %while.42 = (s32[]{:T(128)}, bf16[16,1664]{1,0:T(8,128)(2,1)S(1)}, bf16[128,1664]{1,0:T(8,128)(2,1)S(1)}, pred[]{:T(512)}, s32[]{:T(128)}, /*index=5*/bf16[8,16,...) while((s32[]{:T(128)}, bf16[16,1664]{1,0:T(8,128)(2,1)S(1)}, ...), condition=%wide.region_13.15_spmd, body=%wide.region_6.14_spmd.sunk | while | flops 178327632 | bytes 14285020 | solution.py:157
  638.0 38.0 %reduce-scatter.6.cloned.1.call-done = bf16[1664,16]{1,0:T(8,128)(2,1)} async-done(((bf16[3328,16]{1,0:T(8,128)(2,1)}), bf16[1664,16]{1,0:T(8,128)(2,1)}) %reduce-scatter.6.cloned.1.call-update) | async-done | bytes 53264 | tf_op jit(solution)/shard_map/while
  688.3 15.8 %reduce-scatter.6.cloned.1.call-done = bf16[1664,16]{1,0:T(8,128)(2,1)} async-done(((bf16[3328,16]{1,0:T(8,128)(2,1)}), bf16[1664,16]{1,0:T(8,128)(2,1)}) %reduce-scatter.6.cloned.1.call-update) | async-done | bytes 53264 | tf_op jit(solution)/shard_map/while
  716.5 16.6 %reduce-scatter.6.cloned.1.call-done = bf16[1664,16]{1,0:T(8,128)(2,1)} async-done(((bf16[3328,16]{1,0:T(8,128)(2,1)}), bf16[1664,16]{1,0:T(8,128)(2,1)}) %reduce-scatter.6.cloned.1.call-update) | async-done | bytes 53264 | tf_op jit(solution)/shard_map/while
  745.5 16.6 %reduce-scatter.6.cloned.1.call-done = bf16[1664,16]{1,0:T(8,128)(2,1)} async-done(((bf16[3328,16]{1,0:T(8,128)(2,1)}), bf16[1664,16]{1,0:T(8,128)(2,1)}) %reduce-scatter.6.cloned.1.call-update) | async-done | bytes 53264 | tf_op jit(solution)/shard_map/while
  774.5 16.6 %reduce-scatter.6.cloned.1.call-done = bf16[1664,16]{1,0:T(8,128)(2,1)} async-done(((bf16[3328,16]{1,0:T(8,128)(2,1)}), bf16[1664,16]{1,0:T(8,128)(2,1)}) %reduce-scatter.6.cloned.1.call-update) | async-done | bytes 53264 | tf_op jit(solution)/shard_map/while
  803.5 16.6 %reduce-scatter.6.cloned.1.call-done = bf16[1664,16]{1,0:T(8,128)(2,1)} async-done(((bf16[3328,16]{1,0:T(8,128)(2,1)}), bf16[1664,16]{1,0:T(8,128)(2,1)}) %reduce-scatter.6.cloned.1.call-update) | async-done | bytes 53264 | tf_op jit(solution)/shard_map/while
  832.5 16.6 %reduce-scatter.6.cloned.1.call-done = bf16[1664,16]{1,0:T(8,128)(2,1)} async-done(((bf16[3328,16]{1,0:T(8,128)(2,1)}), bf16[1664,16]{1,0:T(8,128)(2,1)}) %reduce-scatter.6.cloned.1.call-update) | async-done | bytes 53264 | tf_op jit(solution)/shard_map/while
  868.6 9.4 reduce-scatter.6.cloned.1.call-done
  889.0 7.2 conditional.5
  897.6 9.4 reduce-scatter.6.cloned.1.call-done
  926.6 9.4 reduce-scatter.6.cloned.1.call-done
  947.0 7.2 conditional.5
  955.6 8.5 reduce-scatter.6.cloned.1.call-done
  983.7 8.5 reduce-scatter.6.cloned.1.call-done
  1003.1 7.2 conditional.5
  1011.8 7.6 reduce-scatter.6.cloned.1.call-done
  1038.9 7.6 reduce-scatter.6.cloned.1.call-done
  1081.9 11.7 %all_gather.15 = bf16[256,1664]{1,0:T(8,128)(2,1)S(1)} all-gather(bf16[128,1664]{1,0:T(8,128)(2,1)S(1)} %get-tuple-element.673), channel_id=1, replica_groups=mesh['section'=8,'dp'=2,'mp'=2] {'dp'}, dimensions={0}, use_global_device_ids=true | all-gather | bytes 1277952 | tf_op jit(solution)/shard_map/all_gather | solution.py:161
  1094.2 18.2 %convert_bitcast_fusion = (bf16[1,1664,1664]{2,1,0:T(8,128)(2,1)}, f32[1,1664,1664]{2,1,0:T(8,128)}, bf16[1,1664,1664]{2,1,0:T(8,128)(2,1)}) fusion(f32[8,1,1,208,1664]{4,3,2,1,0:T(8,128)} %convert_multiply_fusion.6, f32[8,1,1,208,1664]{4,3,2,1,0:T(8,128)} %convert_multiply_fusion.7, bf16[8,1,1,208,1664]{4,3,2,1,0:T(8,128)(2,1)} %all_to_all.49, ...), kind=kOutput, calls=%fused_computation.52 | convolution fusion | flops 1456439296 | bytes 51544064 | tf_op jit(solution)/shard_map/dot_general | solution.py:159
  (376 shorter events, 528.2 us)
Async XLA Ops:
  169.9 126.0 %all-to-all-start.1 = ((bf16[8,1,1,208,1664]{4,3,2,1,0:T(8,128)(2,1)}), bf16[8,1,1,208,1664]{4,3,2,1,0:T(8,128)(2,1)}, u32[]{:S(2)}, u32[]{:S(2)}) async-start(bf16[8,1,1,208,1664]{4,3,2,1,0:T(8,128)(2,1)} %get-tuple-element.728), calls=%async_computation.2 | async-start | bytes 11075584 | tf_op jit(solution)/shard_map/all_to_all | solution.py:57
  174.7 254.7 %all-gather.2.cloned.1.call-start = ((), (), s32[]{:S(2)}) async-start(), calls=%async_computation.5 | async-start | bytes 16613376 | tf_op jit(solution)/shard_map/all_gather | solution.py:62
  295.9 125.9 %all-to-all-start.3 = ((bf16[8,1,1,208,1664]{4,3,2,1,0:T(8,128)(2,1)}), bf16[8,1,1,208,1664]{4,3,2,1,0:T(8,128)(2,1)}, u32[]{:S(2)}, u32[]{:S(2)}) async-start(bf16[8,1,1,208,1664]{4,3,2,1,0:T(8,128)(2,1)} %get-tuple-element.727), calls=%async_computation.4 | async-start | bytes 11075584 | tf_op jit(solution)/shard_map/all_to_all | solution.py:58
  448.6 6.0 collective-permute-start
  463.6 6.0 collective-permute-start
  493.4 6.0 collective-permute-start
  508.3 6.4 collective-permute-start
  523.6 6.9 collective-permute-start
  539.4 6.9 collective-permute-start
  548.2 13.9 %collective-permute-start = (bf16[16,1664]{1,0:T(8,128)(2,1)S(1)}, bf16[16,1664]{1,0:T(8,128)(2,1)S(1)}, u32[]{:S(2)}, u32[]{:S(2)}) collective-permute-start(bf16[16,1664]{1,0:T(8,128)(2,1)S(1)} %get-tuple-element.861), channel_id=1, source_target_pairs={{0,4},{4,8},{8,12},{12,16},{16,20},{20,24},{24,28},{1,5},{5,9},{9,... | collective-permute-start | bytes 159752 | tf_op jit(solution)/shard_map/while/body/eval_jaxpr/ppermute | solution.py:18
  564.1 6.9 collective-permute-start
  572.9 13.9 %collective-permute-start = (bf16[16,1664]{1,0:T(8,128)(2,1)S(1)}, bf16[16,1664]{1,0:T(8,128)(2,1)S(1)}, u32[]{:S(2)}, u32[]{:S(2)}) collective-permute-start(bf16[16,1664]{1,0:T(8,128)(2,1)S(1)} %get-tuple-element.861), channel_id=1, source_target_pairs={{0,4},{4,8},{8,12},{12,16},{16,20},{20,24},{24,28},{1,5},{5,9},{9,... | collective-permute-start | bytes 159752 | tf_op jit(solution)/shard_map/while/body/eval_jaxpr/ppermute | solution.py:18
  588.7 6.9 collective-permute-start
  597.5 9.8 collective-permute-start
  609.2 6.9 collective-permute-start
  618.0 10.7 collective-permute-start
  631.9 461.7 %all-to-all-start.2 = ((bf16[2,1664,128]{2,1,0:T(8,128)(2,1)}), bf16[2,1664,128]{2,1,0:T(8,128)(2,1)S(1)}, u32[]{:S(2)}, u32[]{:S(2)}) async-start(bf16[2,1664,128]{2,1,0:T(8,128)(2,1)} %bitcast.104), calls=%async_computation.3 | async-start | bytes 1703936 | tf_op jit(solution)/shard_map/all_to_all | solution.py:158
  635.5 40.5 %reduce-scatter.6.cloned.1.call-start = ((), (), s32[]{:S(2)}) async-start(), calls=%async_computation.6 | async-start | bytes 1277952 | tf_op jit(solution)/shard_map/while
  686.0 18.1 %reduce-scatter.6.cloned.1.call-start = ((), (), s32[]{:S(2)}) async-start(), calls=%async_computation.6 | async-start | bytes 1277952 | tf_op jit(solution)/shard_map/while
  714.1 19.0 %reduce-scatter.6.cloned.1.call-start = ((), (), s32[]{:S(2)}) async-start(), calls=%async_computation.6 | async-start | bytes 1277952 | tf_op jit(solution)/shard_map/while
  743.1 19.0 %reduce-scatter.6.cloned.1.call-start = ((), (), s32[]{:S(2)}) async-start(), calls=%async_computation.6 | async-start | bytes 1277952 | tf_op jit(solution)/shard_map/while
  772.1 19.0 %reduce-scatter.6.cloned.1.call-start = ((), (), s32[]{:S(2)}) async-start(), calls=%async_computation.6 | async-start | bytes 1277952 | tf_op jit(solution)/shard_map/while
  801.1 19.0 %reduce-scatter.6.cloned.1.call-start = ((), (), s32[]{:S(2)}) async-start(), calls=%async_computation.6 | async-start | bytes 1277952 | tf_op jit(solution)/shard_map/while
  830.1 19.0 %reduce-scatter.6.cloned.1.call-start = ((), (), s32[]{:S(2)}) async-start(), calls=%async_computation.6 | async-start | bytes 1277952 | tf_op jit(solution)/shard_map/while
  859.1 19.0 %reduce-scatter.6.cloned.1.call-start = ((), (), s32[]{:S(2)}) async-start(), calls=%async_computation.6 | async-start | bytes 1277952 | tf_op jit(solution)/shard_map/while
  888.1 19.0 %reduce-scatter.6.cloned.1.call-start = ((), (), s32[]{:S(2)}) async-start(), calls=%async_computation.6 | async-start | bytes 1277952 | tf_op jit(solution)/shard_map/while
  917.1 19.0 %reduce-scatter.6.cloned.1.call-start = ((), (), s32[]{:S(2)}) async-start(), calls=%async_computation.6 | async-start | bytes 1277952 | tf_op jit(solution)/shard_map/while
  946.1 18.1 %reduce-scatter.6.cloned.1.call-start = ((), (), s32[]{:S(2)}) async-start(), calls=%async_computation.6 | async-start | bytes 1277952 | tf_op jit(solution)/shard_map/while
  974.2 18.1 %reduce-scatter.6.cloned.1.call-start = ((), (), s32[]{:S(2)}) async-start(), calls=%async_computation.6 | async-start | bytes 1277952 | tf_op jit(solution)/shard_map/while
  1002.2 17.2 %reduce-scatter.6.cloned.1.call-start = ((), (), s32[]{:S(2)}) async-start(), calls=%async_computation.6 | async-start | bytes 1277952 | tf_op jit(solution)/shard_map/while
  1029.4 17.2 %reduce-scatter.6.cloned.1.call-start = ((), (), s32[]{:S(2)}) async-start(), calls=%async_computation.6 | async-start | bytes 1277952 | tf_op jit(solution)/shard_map/while
  1056.6 15.3 %reduce-scatter.6.cloned.1.call-start = ((), (), s32[]{:S(2)}) async-start(), calls=%async_computation.6 | async-start | bytes 1277952 | tf_op jit(solution)/shard_map/while
  (18 other events, 225.5 us)
Sparse Core Ops, SparseCore 0:
  177.1 137.2 all-gather.1
  639.2 36.7 reduce-scatter.5
  689.6 14.4 reduce-scatter.5
  717.5 15.6 reduce-scatter.5
  746.5 15.6 reduce-scatter.5
  775.4 15.6 reduce-scatter.5
  804.8 15.2 reduce-scatter.5
  833.8 15.2 reduce-scatter.5
  868.6 9.4 reduce-scatter.5
  897.6 9.4 reduce-scatter.5
  926.6 9.4 reduce-scatter.5
  955.6 8.5 reduce-scatter.5
  983.7 8.5 reduce-scatter.5
  1011.7 7.5 reduce-scatter.5
  1038.9 7.6 reduce-scatter.5
  1066.1 5.7 reduce-scatter.5
where the time goes:
time: 1120 us
  waiting for transfers between devices  536 us (48%)
  blocking collectives  207 us (18%)
  starting transfers between devices  122 us (11%)
  matrix products  121 us (11%)
  other arithmetic  59.1 us (5%)
  local copies, waits for them, and re-layouts  58.1 us (5%)
  between operations  13.9 us (1%)
    while x30, waiting for transfers between devices  204 us
    all_to_all x1, blocking collectives, local(): lax.all_to_all(ordered_w.astype(jnp.bfloat16), 'section', split_axis=0, c...  130 us
    all_to_all x1, waiting for transfers between devices, local(): lax.all_to_all(ordered_m, 'section', split_axis=0, concat_axis=2, tiled=T...  121 us
    all_to_all x1, waiting for transfers between devices, local(): lax.all_to_all(ordered_v, 'section', split_axis=0, concat_axis=2, tiled=T...  114 us
    ppermute x30, starting transfers between devices, from_behind(): return lax.ppermute(value, axis, pairs)  109 us
    ppermute x30, waiting for transfers between devices, from_behind(): return lax.ppermute(value, axis, pairs)  97.4 us
    dot_general x8, matrix products, grad_part(): lax.dot_general(dpre, weight_copy, (((1,), (1,)), ((), ())), preferred_el...  57 us
    dot_general x8, matrix products, layer_forward(): preact = jnp.dot(normed, weight_copy, preferred_element_type=jnp.float32)  46 us
  transfers between devices with their start and end apart: 49, of which 47 were waited for; matrix products, arithmetic and copies ran while one was open for 12% of the time, Pallas kernels for 0%

commit v1 on v0

v1 whole, which is shorter than its diff:
```python
import jax
import jax.numpy as jnp
from jax import lax
from jax.experimental import pallas as pl
from jax.experimental.pallas import tpu as pltpu
from jax.sharding import PartitionSpec as P

eps_norm = 1e-05
beta_one = 0.9
beta_two = 0.95
learn_rate = 0.001
decay_rate = 0.1
adam_eps = 1e-08
step_count = 1000.0

GROUPS = 2
CHUNKS = 2
KERNEL_VMEM = 24 * 1024 * 1024


def turn(value, axis, by):
    count = lax.axis_size(axis)
    return lax.ppermute(value, axis, [(i, (i + by) % count) for i in range(count)])


def after(value, *others):
    return lax.optimization_barrier((value,) + others)[0]


def relocate(pieces):
    moved = lax.all_to_all(pieces, "section", split_axis=0, concat_axis=2, tiled=True)
    return moved.reshape(-1, moved.shape[-1])


def column_cuts(width, parts):
    lanes = width // 128
    edges = [lanes * i // parts * 128 for i in range(parts)] + [width]
    return list(zip(edges[:-1], edges[1:]))


def ordered_cast(inverse, pieces, cuts):
    slots, _, _, rows, width = pieces.shape

    def body(order_ref, in_ref, *out_refs):
        for (lo, hi), out_ref in zip(cuts, out_refs):
            out_ref[...] = in_ref[:, :, :, :, lo:hi].astype(out_ref.dtype)

    def place(i, order_ref):
        return (i, 0, 0, 0, 0)

    return pl.pallas_call(
        body,
        out_shape=[
            jax.ShapeDtypeStruct((slots, 1, 1, rows, hi - lo), jnp.bfloat16) for lo, hi in cuts
        ],
        grid_spec=pltpu.PrefetchScalarGridSpec(
            num_scalar_prefetch=1,
            grid=(slots,),
            in_specs=[pl.BlockSpec((1, 1, 1, rows, width), lambda i, o: (o[i], 0, 0, 0, 0))],
            out_specs=[pl.BlockSpec((1, 1, 1, rows, hi - lo), place) for lo, hi in cuts],
        ),
        compiler_params=pltpu.CompilerParams(vmem_limit_bytes=KERNEL_VMEM),
    )(inverse, pieces)


def adam(features, dpre, master, moment_one, moment_two, row_tile):
    rows, width = moment_one.shape
    depth = dpre.shape[0]
    fix_one = 1.0 - beta_one**step_count
    fix_two = 1.0 - beta_two**step_count

    def body(feature_ref, dpre_ref, w_ref, m_ref, v_ref, new_w_ref, new_m_ref, new_v_ref):
        grad = lax.dot_general(
            feature_ref[...],
            dpre_ref[...],
            (((0,), (0,)), ((), ())),
            preferred_element_type=jnp.float32,
        )
        moment_next = beta_one * m_ref[...].astype(jnp.float32) + (1.0 - beta_one) * grad
        second_next = beta_two * v_ref[...].astype(jnp.float32) + (1.0 - beta_two) * grad * grad
        direction = moment_next / fix_one / (jnp.sqrt(second_next / fix_two) + adam_eps)
        master_rows = w_ref[...].astype(jnp.float32)
        new_w_ref[...] = master_rows - learn_rate * (direction + decay_rate * master_rows)
        new_m_ref[...] = moment_next.astype(jnp.bfloat16)
        new_v_ref[...] = second_next.astype(jnp.bfloat16)

    tile = pl.BlockSpec((row_tile, width), lambda i: (i, 0))
    return pl.pallas_call(
        body,
        grid=(rows // row_tile,),
        in_specs=[
            pl.BlockSpec((depth, row_tile), lambda i: (0, i)),
            pl.BlockSpec((depth, width), lambda i: (0, 0)),
            tile,
            tile,
            tile,
        ],
        out_specs=[tile, tile, tile],
        out_shape=[
            jax.ShapeDtypeStruct((rows, width), jnp.float32),
            jax.ShapeDtypeStruct((rows, width), jnp.bfloat16),
            jax.ShapeDtypeStruct((rows, width), jnp.bfloat16),
        ],
        compiler_params=pltpu.CompilerParams(vmem_limit_bytes=KERNEL_VMEM),
    )(features, dpre, master, moment_one, moment_two)


def local(old_w, old_m, old_v, old_slot_layer, norm_gain, tokens, cotangent):
    sections = lax.axis_size("section")
    replicas = lax.axis_size("dp")
    cores = lax.axis_size("mp")
    section_index = lax.axis_index("section")
    replica_index = lax.axis_index("dp")
    core_index = lax.axis_index("mp")
    full_width = tokens.shape[2]
    half_width = old_w.shape[4]
    row_block = sections * old_w.shape[3]
    tokens = tokens.reshape(-1, full_width)
    cotangent = cotangent.reshape(-1, full_width)
    token_total = tokens.shape[0]
    group_rows = token_total // GROUPS
    layer_ids = jnp.arange(sections, dtype=jnp.int32)
    matches = (old_slot_layer[None, :] == layer_ids[:, None]).astype(jnp.int32)
    inverse = jnp.sum(matches * layer_ids[None, :], axis=1)
    cuts = column_cuts(half_width, CHUNKS)

    own_w = [relocate(piece) for piece in ordered_cast(inverse, old_w, cuts)]
    weight = [lax.all_gather(piece, "dp", axis=0, tiled=True) for piece in own_w]
    ordered_m = jnp.take(old_m, after(inverse, own_w[0]), axis=0)
    moment_one = relocate(after(ordered_m, own_w[-1]))
    ordered_v = jnp.take(old_v, after(inverse, own_w[-1]), axis=0)
    moment_two = relocate(after(ordered_v, moment_one))
    weight = lax.optimization_barrier(jnp.concatenate(weight, axis=1))
    master = lax.optimization_barrier(jnp.concatenate(own_w, axis=1))

    gain_row = norm_gain[0]

    def half_of(value, by=0):
        start = lax.rem(core_index + by, cores) * half_width
        return lax.dynamic_slice_in_dim(value, start, half_width, value.ndim - 1)

    turned = [
        lax.optimization_barrier(
            lax.dynamic_slice_in_dim(
                weight, lax.rem(core_index + by, cores) * half_width, half_width, 0
            ).T
        )
        for by in range(cores)
    ]
    tokens = after(tokens, moment_two)

    def row_scale_of(inputs):
        widened = inputs.astype(jnp.float32)
        return lax.rsqrt(jnp.mean(widened * widened, axis=1, keepdims=True) + eps_norm)

    def normed_of(inputs):
        return (inputs.astype(jnp.float32) * row_scale_of(inputs) * gain_row).astype(jnp.bfloat16)

    def put(stash, value, slot):
        return lax.dynamic_update_index_in_dim(stash, value, slot, 0)

    def get(stash, slot):
        return lax.dynamic_index_in_dim(stash, slot, 0, keepdims=False)

    def slot_of(group):
        return jnp.where((group >= 0) & (group < GROUPS), group, GROUPS)

    def hop(value, tick, by):
        senders = [tick - group for group in range(GROUPS) if 0 <= tick - group < sections - 1]
        pairs = [(s, s + 1) for s in senders]
        if by < 0:
            pairs = [(sections - 1 - s, sections - 2 - s) for s in senders]
        return lax.ppermute(value, "section", pairs)

    acts = jnp.zeros((GROUPS + 1, group_rows, full_width), jnp.bfloat16)
    preacts = jnp.zeros((GROUPS + 1, group_rows, half_width), jnp.float32)
    ticks = GROUPS + sections - 1
    arriving = jnp.zeros((group_rows, full_width), jnp.bfloat16)
    for tick in range(ticks):
        slot = slot_of(tick - section_index)
        inputs = arriving
        if tick < GROUPS:
            entry = tokens[tick * group_rows : (tick + 1) * group_rows]
            inputs = jnp.where(section_index == 0, entry, arriving)
        preact = jnp.dot(normed_of(inputs), weight, preferred_element_type=jnp.float32)
        acts = put(acts, inputs, slot)
        preacts = put(preacts, preact, slot)
        if tick < ticks - 1:
            output = (half_of(inputs).astype(jnp.float32) + jax.nn.silu(preact)).astype(
                jnp.bfloat16
            )
            moved = hop(output, tick, 1)
            arriving = lax.all_gather(moved, "mp", axis=1, tiled=True)

    normed_all = normed_of(acts[:GROUPS].reshape(token_total, full_width))
    features = []
    for by in range(replicas):
        block = lax.rem(replica_index + by, replicas) * row_block
        part = lax.dynamic_slice_in_dim(normed_all, block, row_block, 1)
        features.append(turn(part, "dp", by) if by else part)
    features = jnp.concatenate(features, axis=0)

    sigmoid_value = jax.nn.sigmoid(preacts)
    slopes = lax.optimization_barrier(
        sigmoid_value * (1.0 + preacts * (1.0 - sigmoid_value))
    )
    dpres = jnp.zeros((GROUPS + 1, group_rows, half_width), jnp.bfloat16)
    arriving = jnp.zeros((group_rows, half_width), jnp.bfloat16)
    for tick in range(ticks):
        slot = slot_of(tick - (sections - 1 - section_index))
        slope = get(slopes, slot)
        preact = get(preacts, slot)
        inputs = get(acts, slot)
        row_scale = row_scale_of(inputs)
        scaled = [half_of(gain_row, by) * row_scale for by in range(cores)]
        pulled = [
            half_of(inputs, by).astype(jnp.float32) * (row_scale * row_scale / full_width)
            for by in range(cores)
        ]
        slope, preact, scaled, pulled = lax.optimization_barrier((slope, preact, scaled, pulled))
        upstream = arriving
        if tick < GROUPS:
            seed = cotangent[tick * group_rows : (tick + 1) * group_rows]
            upstream = jnp.where(section_index == sections - 1, half_of(seed), arriving)
        dpre = (upstream.astype(jnp.float32) * slope).astype(jnp.bfloat16)
        dpres = put(dpres, dpre, slot)
        if tick == ticks - 1:
            break
        stat = jnp.sum(dpre.astype(jnp.float32) * preact, axis=1, keepdims=True)
        total = upstream.astype(jnp.float32)
        for by in reversed(range(cores)):
            part = (
                scaled[by] * jnp.dot(dpre, turned[by], preferred_element_type=jnp.float32)
                - pulled[by] * stat
            )
            if by:
                part = turn(part.astype(jnp.bfloat16), "mp", by).astype(jnp.float32)
            total = total + part
        arriving = hop(total.astype(jnp.bfloat16), tick, -1)

    dpre_all = dpres[:GROUPS].reshape(token_total, half_width)
    dpre_all = jnp.concatenate(
        [turn(dpre_all, "dp", by) if by else dpre_all for by in range(replicas)], axis=0
    )
    row_tile = 128 if row_block % 128 == 0 else row_block
    updated = adam(features, dpre_all, master, moment_one, moment_two, row_tile)
    return tuple(value[None] for value in updated)


def solution(mesh):
    placed = (
        P(None, "dp", "section", None, "mp"),
        P(None, "dp", "section", None, "mp"),
        P(None, "dp", "section", None, "mp"),
        P(),
        P("section", None),
        P(None, "dp", None),
        P(None, "dp", None),
    )
    return jax.shard_map(
        local,
        mesh=mesh,
        in_specs=placed,
        out_specs=(P("section", "dp", "mp"), P("section", "dp", "mp"), P("section", "dp", "mp")),
        check_vma=False,
    )
```

time: 1120 us -> 713 us (0.64)
  waiting for transfers between devices: 536 us -> 409 us
  blocking collectives: 207 us -> 82.6 us
  starting transfers between devices: 122 us -> 38.2 us
  matrix products: 121 us -> 60.8 us
  local copies, waits for them, and re-layouts: 58.1 us -> 33 us
  Pallas kernels: 0 us -> 23.1 us
  other arithmetic: 59.1 us -> 40.2 us
    while x30 -> x0, waiting for transfers between devices: 204 us -> none
    ppermute x30 -> x26, starting transfers between devices: 109 us -> 25 us  [the longest x16 20.3 us: hop(): return lax.ppermute(value, 'section', pairs)]
    all_gather x1 -> x2, waiting for transfers between devices: 0.01 us -> 78.5 us  [local(): lax.all_gather(piece, 'dp', axis=0, tiled=True)]
    all_to_all x1, blocking collectives: 130 us -> 65.3 us  [relocate(): lax.all_to_all(pieces, 'section', split_axis=0, concat_axis=2, tiled=True)]
    dot_general x17 -> x25, matrix products: 121 us -> 60.8 us  [the longest x16 37.4 us: local(): jnp.dot(dpre, turned[by], preferred_element_type=jnp.float32)]
    all_to_all x3, waiting for transfers between devices: 234 us -> 197 us  [relocate(): lax.all_to_all(pieces, 'section', split_axis=0, concat_axis=2, tiled=True)]
    while x31 -> x0, local copies, waits for them, and re-layouts: 37 us -> none
    psum x15 -> x0, blocking collectives: 37 us -> none  [backward_tick(): row_stat = lax.psum(stat_part, 'mp') / full_width]
  transfers between devices with their start and end apart: 49 -> 31, of which waited for: 47 -> 17; matrix products, arithmetic and copies ran while one was open for 12% -> 7% of each run, Pallas kernels for 0% -> 0%
where the time goes in v1:
time: 713 us; the launch traced here: 703 us
  waiting for transfers between devices  409 us (57%)
  blocking collectives  82.6 us (12%)
  matrix products  60.8 us (9%)
  other arithmetic  40.2 us (6%)
  starting transfers between devices  38.2 us (5%)
  local copies, waits for them, and re-layouts  33 us (5%)
  Pallas kernels  23.1 us (3%)
  between operations  16 us (2%)
    all_to_all x3, waiting for transfers between devices, relocate(): lax.all_to_all(pieces, 'section', split_axis=0, concat_axis=2, tiled=True)  197 us
    ppermute x16, waiting for transfers between devices, hop(): return lax.ppermute(value, 'section', pairs)  116 us
    all_gather x2, waiting for transfers between devices, local(): lax.all_gather(piece, 'dp', axis=0, tiled=True)  78.5 us
    all_to_all x1, blocking collectives, relocate(): lax.all_to_all(pieces, 'section', split_axis=0, concat_axis=2, tiled=True)  65.3 us
    dot_general x16, matrix products, local(): jnp.dot(dpre, turned[by], preferred_element_type=jnp.float32)  37.4 us
    dot_general x9, matrix products, local(): jnp.dot(normed_of(inputs), weight, preferred_element_type=jnp.float32)  23.5 us
    ppermute x16, starting transfers between devices, hop(): return lax.ppermute(value, 'section', pairs)  20.3 us
    pallas_call x1, Pallas kernels, adam(): pl.pallas_call(body, grid=(rows // row_tile,), in_specs=[pl.BlockSpec((de...  19.2 us
  transfers between devices with their start and end apart: 31, of which 17 were waited for; matrix products, arithmetic and copies ran while one was open for 7% of the time, Pallas kernels for 0%

profile of v1, /device:TPU:0, one launch (start us, length us, event | category | flops | bytes accessed | tf_op | source)
XLA Modules:
  0.0 703.2 jit_solution(9282801266630290238)
XLA Ops:
  7.9 4.1 copy-done
  12.1 3.9 shard_map.94
  16.0 65.3 %all_to_all.16 = bf16[8,1,1,208,768]{4,3,2,1,0:T(8,128)(2,1)} all-to-all(bf16[8,1,1,208,768]{4,3,2,1,0:T(8,128)(2,1)S(1)} %get-tuple-element.64), channel_id=1, replica_groups=mesh['section'=8,'dp'=2,'mp'=2] {'section'}, dimensions={0} | all-to-all | bytes 5111808 | tf_op jit(solution)/shard_map/all_to_all | solution.py:31
  81.3 3.6 all-to-all-start
  85.0 66.8 %all-to-all-done = bf16[8,1,1,208,896]{4,3,2,1,0:T(8,128)(2,1)S(1)} async-done(((bf16[8,1,1,208,896]{4,3,2,1,0:T(8,128)(2,1)}), bf16[8,1,1,208,896]{4,3,2,1,0:T(8,128)(2,1)S(1)}, u32[]{:S(2)}, u32[]{:S(2)}) %all-to-all-start) | async-done | bytes 2981920 | tf_op jit(solution)/shard_map/all_to_all | solution.py:31
  151.8 7.2 %gather_fusion.1 = bf16[8,208,1664]{2,1,0:T(8,128)(2,1)} fusion(bf16[8,208,1664]{2,1,0:T(8,128)(2,1)} %bitcast.224, s32[1024]{0:T(1024)S(1)} %pad_clamp_fusion), kind=kCustom, calls=%fused_computation.1.clone | custom fusion | bytes 11075616 | tf_op jit(solution)/shard_map/jit(_take)/gather | solution.py:129
  159.0 5.6 bitcast_select_fusion
  164.7 4.7 all-to-all-start.2
  170.1 6.2 gather_fusion
  176.3 6.0 bitcast_select_fusion.1
  182.3 108.3 %all-to-all-done.2 = bf16[8,1,1,208,1664]{4,3,2,1,0:T(8,128)(2,1)} async-done(((bf16[8,1,1,208,1664]{4,3,2,1,0:T(8,128)(2,1)}), bf16[8,1,1,208,1664]{4,3,2,1,0:T(8,128)(2,1)}, u32[]{:S(2)}, u32[]{:S(2)}) %all-to-all-start.2) | async-done | bytes 5537824 | tf_op jit(solution)/shard_map/all_to_all | solution.py:31
  290.6 4.8 all-to-all-start.3
  297.4 78.5 %all-gather.5.cloned.1.call-done = bf16[3328,896]{1,0:T(8,128)(2,1)} async-done(((bf16[1664,896]{1,0:T(8,128)(2,1)}), bf16[3328,896]{1,0:T(8,128)(2,1)}) %all-gather.5.cloned.1.call-update) | async-done | bytes 5963792 | tf_op jit(solution)/shard_map/all_gather | solution.py:128
  375.8 9.5 %pad_maximum_fusion = bf16[3328,1664]{1,0:T(8,128)(2,1)} fusion(bf16[3328,896]{1,0:T(8,128)(2,1)} %all-gather.5.cloned.1.call-done, bf16[3328,768]{1,0:T(8,128)(2,1)} %all-gather.3.cloned.1.call-done), kind=kLoop, calls=%fused_computation.2 | loop fusion | flops 22151168 | bytes 22151168 | tf_op jit(solution)/shard_map/concatenate | solution.py:133
  385.4 9.4 %dynamic-slice_bitcast_fusion = (bf16[1664,1664]{0,1:T(8,128)(2,1)}, bf16[1664,1664]{0,1:T(8,128)(2,1)}) fusion(bf16[3328,1664]{1,0:T(8,128)(2,1)} %pad_maximum_fusion, s32[]{:T(128)S(6)} %select_n.271, s32[]{:T(128)S(6)} %select_n.295), kind=kLoop, calls=%fused_computation.6 | loop fusion | bytes 22151176 | tf_op jit(solution)/shard_map/transpose | solution.py:146
  394.7 21.9 %all-to-all-done.3 = bf16[8,1,1,208,1664]{4,3,2,1,0:T(8,128)(2,1)} async-done(((bf16[8,1,1,208,1664]{4,3,2,1,0:T(8,128)(2,1)}), bf16[8,1,1,208,1664]{4,3,2,1,0:T(8,128)(2,1)}, u32[]{:S(2)}, u32[]{:S(2)}) %all-to-all-start.3) | async-done | bytes 5537824 | tf_op jit(solution)/shard_map/all_to_all | solution.py:31
  416.9 6.4 add_convert_fusion.7
  423.3 3.4 collective-permute-start
  427.0 3.4 collective-permute-done
  434.9 4.4 collective-permute-start.1
  439.4 4.7 collective-permute-done.1
  475.7 2.3 all_gather.39
  484.7 2.8 broadcast_multiply_fusion.1
  487.5 4.5 convert_multiply_fusion.26
  505.7 4.7 fusion.22
  512.0 3.4 fusion.62
  518.4 4.7 fusion.21
  524.6 3.3 fusion.65
  550.6 99.8 %collective-permute-done.22 = bf16[64,1664]{1,0:T(8,128)(2,1)S(1)} collective-permute-done((bf16[64,1664]{1,0:T(8,128)(2,1)S(1)}, bf16[64,1664]{1,0:T(8,128)(2,1)S(1)}, u32[]{:S(2)}, u32[]{:S(2)}) %collective-permute-start.22) | collective-permute-done | bytes 213024 | tf_op jit(solution)/shard_map/ppermute | solution.py:173
  657.0 8.1 %collective-permute-done.24 = bf16[64,1664]{1,0:T(8,128)(2,1)S(1)} collective-permute-done((bf16[64,1664]{1,0:T(8,128)(2,1)S(1)}, bf16[64,1664]{1,0:T(8,128)(2,1)S(1)}, u32[]{:S(2)}, u32[]{:S(2)}) %collective-permute-start.24) | collective-permute-done | bytes 213024 | tf_op jit(solution)/shard_map/ppermute | solution.py:173
  670.0 6.6 collective-permute-done.25
  676.7 19.2 %shard_map.95 = (f32[1664,1664]{1,0:T(8,128)}, bf16[1664,1664]{1,0:T(8,128)(2,1)}, bf16[1664,1664]{1,0:T(8,128)(2,1)}) custom-call(bf16[256,1664]{1,0:T(8,128)(2,1)S(1)} %pad_maximum_fusion.2.feature_ref, bf16[256,1664]{1,0:T(8,128)(2,1)S(1)} %pad_maximum_fusion.3.dpre_ref, bf16[1664,1664]{1,0:T(8,128)(2,1)S(1)} %pad_maximum_fusion.1.w_ref, ...), custom_call_target="tpu_custom_call" | custom-call | tf_op jit(solution)/shard_map/pallas_call | solution.py:88
  (274 shorter events, 99.7 us)
Async XLA Ops:
  81.3 70.4 %all-to-all-start = ((bf16[8,1,1,208,896]{4,3,2,1,0:T(8,128)(2,1)}), bf16[8,1,1,208,896]{4,3,2,1,0:T(8,128)(2,1)S(1)}, u32[]{:S(2)}, u32[]{:S(2)}) async-start(bf16[8,1,1,208,896]{4,3,2,1,0:T(8,128)(2,1)} %get-tuple-element.62), calls=%async_computation | async-start | bytes 5963776 | tf_op jit(solution)/shard_map/all_to_all | solution.py:31
  164.7 125.9 %all-to-all-start.2 = ((bf16[8,1,1,208,1664]{4,3,2,1,0:T(8,128)(2,1)}), bf16[8,1,1,208,1664]{4,3,2,1,0:T(8,128)(2,1)}, u32[]{:S(2)}, u32[]{:S(2)}) async-start(bf16[8,1,1,208,1664]{4,3,2,1,0:T(8,128)(2,1)} %bitcast_select_fusion), calls=%async_computation.2 | async-start | bytes 11075584 | tf_op jit(solution)/shard_map/all_to_all | solution.py:31
  169.4 128.0 %all-gather.3.cloned.1.call-start = ((), (), s32[]{:S(2)}) async-start(), calls=%async_computation.4 | async-start | bytes 7667712 | tf_op jit(solution)/shard_map/all_gather | solution.py:128
  290.6 126.0 %all-to-all-start.3 = ((bf16[8,1,1,208,1664]{4,3,2,1,0:T(8,128)(2,1)}), bf16[8,1,1,208,1664]{4,3,2,1,0:T(8,128)(2,1)}, u32[]{:S(2)}, u32[]{:S(2)}) async-start(bf16[8,1,1,208,1664]{4,3,2,1,0:T(8,128)(2,1)} %bitcast_select_fusion.1), calls=%async_computation.3 | async-start | bytes 11075584 | tf_op jit(solution)/shard_map/all_to_all | solution.py:31
  295.4 80.4 %all-gather.5.cloned.1.call-start = ((), (), s32[]{:S(2)}) async-start(), calls=%async_computation.5 | async-start | bytes 8945664 | tf_op jit(solution)/shard_map/all_gather | solution.py:128
  423.3 7.1 %collective-permute-start = (bf16[64,1664]{1,0:T(8,128)(2,1)S(1)}, bf16[64,1664]{1,0:T(8,128)(2,1)S(1)}, u32[]{:S(2)}, u32[]{:S(2)}) collective-permute-start(bf16[64,1664]{1,0:T(8,128)(2,1)S(1)} %get-tuple-element.243), channel_id=1, source_target_pairs={{0,4},{1,5},{2,6},{3,7}} | collective-permute-start | bytes 638984 | tf_op jit(solution)/shard_map/ppermute | solution.py:173
  434.9 9.2 %collective-permute-start.1 = (bf16[64,1664]{1,0:T(8,128)(2,1)S(1)}, bf16[64,1664]{1,0:T(8,128)(2,1)S(1)}, u32[]{:S(2)}, u32[]{:S(2)}) collective-permute-start(bf16[64,1664]{1,0:T(8,128)(2,1)S(1)} %get-tuple-element.245), channel_id=1, source_target_pairs={{4,8},{0,4},{5,9},{1,5},{6,10},{2,6},{7,11},{3,7}} | collective-permute-start | bytes 638984 | tf_op jit(solution)/shard_map/ppermute | solution.py:173
  448.6 0.8 collective-permute-start.2
  454.0 0.8 collective-permute-start.3
  459.2 0.8 collective-permute-start.4
  464.4 0.8 collective-permute-start.5
  469.7 0.8 collective-permute-start.6
  474.9 0.8 collective-permute-start.7
  494.0 1.5 collective-permute-start.9
  497.3 0.7 collective-permute-start.10
  500.0 1.5 collective-permute-start.11
  503.3 1.0 collective-permute-start.12
  510.4 1.5 collective-permute-start.13
  515.4 1.6 collective-permute-start.14
  523.1 1.5 collective-permute-start.15
  527.9 3.2 collective-permute-start.16
  529.6 139.4 %collective-permute-start.8 = (bf16[128,1664]{1,0:T(8,128)(2,1)}, bf16[128,1664]{1,0:T(8,128)(2,1)}, u32[]{:S(2)}, u32[]{:S(2)}) collective-permute-start(bf16[128,1664]{1,0:T(8,128)(2,1)} %get-tuple-element.202), channel_id=1, source_target_pairs={{0,2},{2,0},{1,3},{3,1},{4,6},{6,4},{5,7},{7,5},{8,10},{10,8},{9,1... | collective-permute-start | bytes 1277960 | tf_op jit(solution)/shard_map/ppermute | solution.py:23
  533.1 1.5 collective-permute-start.17
  536.4 0.8 collective-permute-start.18
  539.3 1.5 collective-permute-start.19
  542.6 0.8 collective-permute-start.20
  545.5 105.1 %copy-start.21 = (f32[64,1664]{1,0:T(8,128)S(1)}, f32[64,1664]{1,0:T(8,128)}, u32[]{:S(2)}) copy-start(f32[64,1664]{1,0:T(8,128)} %get-tuple-element.112) | copy-start | bytes 1277956
  545.5 1.5 collective-permute-start.21
  548.9 101.5 %collective-permute-start.22 = (bf16[64,1664]{1,0:T(8,128)(2,1)S(1)}, bf16[64,1664]{1,0:T(8,128)(2,1)S(1)}, u32[]{:S(2)}, u32[]{:S(2)}) collective-permute-start(bf16[64,1664]{1,0:T(8,128)(2,1)S(1)} %fusion.74), channel_id=1, source_target_pairs={{4,0},{8,4},{5,1},{9,5},{6,2},{10,6},{7,3},{11,7}} | collective-permute-start | bytes 638984 | tf_op jit(solution)/shard_map/ppermute | solution.py:173
  652.4 1.5 collective-permute-start.23
  655.7 9.5 %collective-permute-start.24 = (bf16[64,1664]{1,0:T(8,128)(2,1)S(1)}, bf16[64,1664]{1,0:T(8,128)(2,1)S(1)}, u32[]{:S(2)}, u32[]{:S(2)}) collective-permute-start(bf16[64,1664]{1,0:T(8,128)(2,1)S(1)} %fusion.77), channel_id=1, source_target_pairs={{4,0},{5,1},{6,2},{7,3}} | collective-permute-start | bytes 638984 | tf_op jit(solution)/shard_map/ppermute | solution.py:173
  665.2 11.4 %collective-permute-start.25 = (bf16[128,1664]{1,0:T(8,128)(2,1)S(1)}, bf16[128,1664]{1,0:T(8,128)(2,1)S(1)}, u32[]{:S(2)}, u32[]{:S(2)}) collective-permute-start(bf16[128,1664]{1,0:T(8,128)(2,1)S(1)} %bitcast.228), channel_id=1, source_target_pairs={{0,2},{2,0},{1,3},{3,1},{4,6},{6,4},{5,7},{7,5},{8,10},{10,8},{9,1... | collective-permute-start | bytes 1277960 | tf_op jit(solution)/shard_map/ppermute | solution.py:23
  (52 other events, 888.1 us)
Sparse Core Ops, SparseCore 0:
  171.8 68.3 all-gather.2
  297.8 77.9 all-gather.4

commit v2 on v1

v2 whole, which is shorter than its diff:
```python
import jax
import jax.numpy as jnp
from jax import lax
from jax.experimental import pallas as pl
from jax.experimental.pallas import tpu as pltpu
from jax.sharding import PartitionSpec as P

eps_norm = 1e-05
beta_one = 0.9
beta_two = 0.95
learn_rate = 0.001
decay_rate = 0.1
adam_eps = 1e-08
step_count = 1000.0

GROUPS = 2
EARLY = 2
STEP_VMEM = 16 * 1024 * 1024
ADAM_VMEM = 20 * 1024 * 1024


def turn(value, axis, by):
    count = lax.axis_size(axis)
    return lax.ppermute(value, axis, [(i, (i + by) % count) for i in range(count)])


def zero_after(value):
    first = lax.slice(value, (0,) * value.ndim, (1,) * value.ndim).reshape(())
    return jnp.minimum((first > 0).astype(jnp.int32), 0)


def relocate(pieces):
    moved = lax.all_to_all(pieces, "section", split_axis=0, concat_axis=2, tiled=True)
    return moved.reshape(-1, moved.shape[-1])


def ordered_copy(picks, pieces):
    slots, _, _, rows, width = pieces.shape

    def body(pick_ref, in_ref, out_ref):
        out_ref[...] = in_ref[...].astype(out_ref.dtype)

    return pl.pallas_call(
        body,
        out_shape=jax.ShapeDtypeStruct((picks.shape[0], 1, 1, rows, width), jnp.bfloat16),
        grid_spec=pltpu.PrefetchScalarGridSpec(
            num_scalar_prefetch=1,
            grid=(picks.shape[0],),
            in_specs=[pl.BlockSpec((1, 1, 1, rows, width), lambda i, p: (p[i], 0, 0, 0, 0))],
            out_specs=pl.BlockSpec((1, 1, 1, rows, width), lambda i, p: (i, 0, 0, 0, 0)),
        ),
        compiler_params=pltpu.CompilerParams(vmem_limit_bytes=STEP_VMEM),
    )(picks, pieces)


def resident(array):
    def body(in_ref, out_ref, sem):
        copy = pltpu.make_async_copy(in_ref, out_ref, sem)
        copy.start()
        copy.wait()

    return pl.pallas_call(
        body,
        out_shape=pltpu.VMEM(array.shape, array.dtype),
        in_specs=[pl.BlockSpec(memory_space=pl.ANY)],
        out_specs=pl.BlockSpec(memory_space=pltpu.VMEM),
        scratch_shapes=[pltpu.SemaphoreType.DMA],
        compiler_params=pltpu.CompilerParams(vmem_limit_bytes=STEP_VMEM),
    )(in_hbm(array))


def picked_pieces(picks, pieces):
    _, _, _, rows, width = pieces.shape
    count = picks.shape[0]

    def body(pick_ref, in_ref, *refs):
        out_refs, sems = refs[:count], refs[count]
        copies = [
            pltpu.make_async_copy(in_ref.at[pick_ref[i], 0, 0], out_refs[i], sems.at[i])
            for i in range(count)
        ]
        for copy in copies:
            copy.start()
        for copy in copies:
            copy.wait()

    return pl.pallas_call(
        body,
        out_shape=[jax.ShapeDtypeStruct((rows, width), pieces.dtype)] * count,
        in_specs=[pl.BlockSpec(memory_space=pltpu.SMEM), pl.BlockSpec(memory_space=pl.ANY)],
        out_specs=[pl.BlockSpec(memory_space=pl.ANY)] * count,
        scratch_shapes=[pltpu.SemaphoreType.DMA((count,))],
        compiler_params=pltpu.CompilerParams(vmem_limit_bytes=STEP_VMEM),
    )(picks, pieces)


def tiles_of(width):
    return [(start, min(256, width - start)) for start in range(0, width, 256)]


def in_vmem(array):
    return pltpu.with_memory_space_constraint(array, pltpu.VMEM)


def in_hbm(array):
    return pltpu.with_memory_space_constraint(array, pltpu.HBM)


WHOLE = pl.BlockSpec(memory_space=pltpu.VMEM)
SCALAR = pl.BlockSpec(memory_space=pltpu.SMEM)
ANYWHERE = pl.BlockSpec(memory_space=pl.ANY)


def forward_step(core, inputs, gain, weight):
    rows, full_width = inputs.shape
    half_width = weight.shape[1]

    def body(core_ref, x_ref, gain_ref, w_ref, out_ref, normed_ref, preact_ref, scale_ref, _):
        wide = x_ref[...].astype(jnp.float32)
        scale = lax.rsqrt(jnp.mean(wide * wide, axis=1, keepdims=True) + eps_norm)
        normed = (wide * scale * gain_ref[...]).astype(jnp.bfloat16)
        normed_ref[...] = normed
        scale_ref[...] = jnp.broadcast_to(scale, scale_ref.shape)
        offset = pl.multiple_of(core_ref[0] * half_width, 128)
        for start, size in tiles_of(half_width):
            preact = jnp.dot(
                normed, w_ref[:, start : start + size], preferred_element_type=jnp.float32
            )
            preact_ref[:, start : start + size] = preact
            own = x_ref[:, pl.ds(pl.multiple_of(offset + start, 128), size)].astype(jnp.float32)
            silu = preact / (1.0 + jnp.exp(-preact))
            out_ref[:, start : start + size] = (own + silu).astype(jnp.bfloat16)

    return pl.pallas_call(
        body,
        in_specs=[SCALAR, WHOLE, WHOLE, WHOLE],
        out_specs=[WHOLE] * 5,
        out_shape=[
            jax.ShapeDtypeStruct((rows, half_width), jnp.bfloat16),
            jax.ShapeDtypeStruct((rows, full_width), jnp.bfloat16),
            jax.ShapeDtypeStruct((rows, half_width), jnp.float32),
            jax.ShapeDtypeStruct((rows, 128), jnp.float32),
            pltpu.VMEM(weight.shape, weight.dtype),
        ],
        input_output_aliases={3: 4},
        compiler_params=pltpu.CompilerParams(vmem_limit_bytes=STEP_VMEM),
    )(core, inputs, gain, in_vmem(weight))


def pull_back(start, dpre, stat, w_ref, x_ref, gain_ref, scale_ref, size, width):
    cols = pl.ds(pl.multiple_of(start, 128), size)
    product = lax.dot_general(
        dpre, w_ref[cols, :], (((1,), (1,)), ((), ())), preferred_element_type=jnp.float32
    )
    scale = scale_ref[:, :1]
    return scale * (
        gain_ref[:, cols] * product - x_ref[:, cols].astype(jnp.float32) * (scale * stat / width)
    )


def backward_away(core, upstream, slope, preact, inputs, row_scale, gain, weight):
    rows, full_width = inputs.shape
    half_width = weight.shape[1]

    def body(
        core_ref, up_ref, slope_ref, preact_ref, x_ref, scale_ref, gain_ref, w_ref,
        dpre_ref, stat_ref, away_ref, _,
    ):
        dpre = (up_ref[...].astype(jnp.float32) * slope_ref[...]).astype(jnp.bfloat16)
        dpre_ref[...] = dpre
        stat = jnp.sum(dpre.astype(jnp.float32) * preact_ref[...], axis=1, keepdims=True)
        stat_ref[...] = jnp.broadcast_to(stat, stat_ref.shape)
        offset = pl.multiple_of(core_ref[0] * half_width, 128)
        for start, size in tiles_of(half_width):
            away_ref[:, start : start + size] = pull_back(
                offset + start, dpre, stat, w_ref, x_ref, gain_ref, scale_ref, size, full_width
            ).astype(jnp.bfloat16)

    return pl.pallas_call(
        body,
        in_specs=[SCALAR] + [WHOLE] * 7,
        out_specs=[WHOLE] * 4,
        out_shape=[
            jax.ShapeDtypeStruct((rows, half_width), jnp.bfloat16),
            jax.ShapeDtypeStruct((rows, 128), jnp.float32),
            jax.ShapeDtypeStruct((rows, half_width), jnp.bfloat16),
            pltpu.VMEM(weight.shape, weight.dtype),
        ],
        input_output_aliases={7: 3},
        compiler_params=pltpu.CompilerParams(vmem_limit_bytes=STEP_VMEM),
    )(core, upstream, slope, preact, inputs, row_scale, gain, in_vmem(weight))


def backward_home(core, upstream, dpre, stat, inputs, row_scale, gain, weight):
    rows, full_width = inputs.shape
    half_width = weight.shape[1]

    def body(core_ref, up_ref, dpre_ref, stat_ref, x_ref, scale_ref, gain_ref, w_ref, home_ref, _):
        dpre = dpre_ref[...]
        offset = pl.multiple_of(core_ref[0] * half_width, 128)
        for start, size in tiles_of(half_width):
            home_ref[:, start : start + size] = up_ref[:, start : start + size].astype(
                jnp.float32
            ) + pull_back(
                offset + start, dpre, stat_ref[:, :1], w_ref, x_ref, gain_ref, scale_ref, size, full_width
            )

    return pl.pallas_call(
        body,
        in_specs=[SCALAR] + [WHOLE] * 7,
        out_specs=[WHOLE, WHOLE],
        out_shape=[
            jax.ShapeDtypeStruct((rows, half_width), jnp.float32),
            pltpu.VMEM(weight.shape, weight.dtype),
        ],
        input_output_aliases={7: 1},
        compiler_params=pltpu.CompilerParams(vmem_limit_bytes=STEP_VMEM),
    )(core, upstream, dpre, stat, inputs, row_scale, gain, in_vmem(weight))


def adam(row_order, sides, features, dpre, master, moment_one, moment_two):
    blocks, rows, width = moment_one.shape
    depth = dpre.shape[0]
    strip = 16 if rows % 16 == 0 else rows
    fix_one = 1.0 - beta_one**step_count
    fix_two = 1.0 - beta_two**step_count

    def body(order_ref, side_ref, feature_ref, dpre_ref, w_ref, m_ref, *refs):
        second_refs, refs = refs[:blocks], refs[blocks:]
        new_w_ref, new_m_ref, new_v_ref, grad_ref, v_ref, sems = refs
        block = pl.program_id(0)

        def fetch(k):
            source = second_refs[k].at[side_ref[k]] if k else second_refs[k]
            return pltpu.make_async_copy(source, v_ref.at[k % 2], sems.at[k % 2])

        @pl.when(block == 0)
        def _():
            fetch(0).start()

        for k in range(blocks):

            @pl.when(block == k)
            def _(k=k):
                if k + 1 < blocks:
                    fetch(k + 1).start()
                fetch(k).wait()

        now = lax.rem(block, 2)
        grad_ref[...] = jnp.dot(
            feature_ref[0], dpre_ref[...], preferred_element_type=jnp.float32
        )

        def step(index, carry):
            part = pl.ds(index * strip, strip)
            grad = grad_ref[part, :]
            moment_next = beta_one * m_ref[0, part, :].astype(jnp.float32) + (1.0 - beta_one) * grad
            second_next = (
                beta_two * v_ref[now, part, :].astype(jnp.float32) + (1.0 - beta_two) * grad * grad
            )
            scaled = second_next / fix_two
            root = scaled * lax.rsqrt(scaled)
            direction = moment_next / fix_one * pl.reciprocal(root + adam_eps, approx=True)
            rows_w = w_ref[0, part, :].astype(jnp.float32)
            new_w_ref[0, part, :] = rows_w - learn_rate * (direction + decay_rate * rows_w)
            new_m_ref[0, part, :] = moment_next.astype(jnp.bfloat16)
            new_v_ref[0, part, :] = second_next.astype(jnp.bfloat16)
            return carry

        lax.fori_loop(0, rows // strip, step, 0)

    def placed(i, order_ref, side_ref):
        return (order_ref[i], 0, 0)

    tile = pl.BlockSpec((1, rows, width), placed)
    return pl.pallas_call(
        body,
        grid_spec=pltpu.PrefetchScalarGridSpec(
            num_scalar_prefetch=2,
            grid=(blocks,),
            in_specs=[
                pl.BlockSpec((1, rows, depth), placed),
                pl.BlockSpec((depth, width), lambda i, o, s: (0, 0)),
                tile,
                tile,
            ]
            + [pl.BlockSpec(memory_space=pl.ANY)] * blocks,
            out_specs=[tile, tile, tile],
            scratch_shapes=[
                pltpu.VMEM((rows, width), jnp.float32),
                pltpu.VMEM((2, rows, width), jnp.bfloat16),
                pltpu.SemaphoreType.DMA((2,)),
            ],
        ),
        out_shape=[
            jax.ShapeDtypeStruct((blocks, rows, width), jnp.float32),
            jax.ShapeDtypeStruct((blocks, rows, width), jnp.bfloat16),
            jax.ShapeDtypeStruct((blocks, rows, width), jnp.bfloat16),
        ],
        compiler_params=pltpu.CompilerParams(vmem_limit_bytes=ADAM_VMEM),
    )(
        row_order,
        sides,
        features,
        dpre,
        in_hbm(master),
        in_hbm(moment_one),
        *[in_hbm(piece) for piece in moment_two],
    )


def local(old_w, old_m, old_v, old_slot_layer, norm_gain, tokens, cotangent):
    sections = lax.axis_size("section")
    replicas = lax.axis_size("dp")
    cores = lax.axis_size("mp")
    section_index = lax.axis_index("section")
    replica_index = lax.axis_index("dp")
    core_index = lax.axis_index("mp")
    full_width = tokens.shape[2]
    half_width = old_w.shape[4]
    row_block = sections * old_w.shape[3]
    tokens = tokens.reshape(-1, full_width)
    cotangent = cotangent.reshape(-1, full_width)
    token_total = tokens.shape[0]
    group_rows = token_total // GROUPS
    layer_ids = jnp.arange(sections, dtype=jnp.int32)
    matches = (old_slot_layer[None, :] == layer_ids[:, None]).astype(jnp.int32)
    inverse = jnp.sum(matches * layer_ids[None, :], axis=1)
    own_w = relocate(ordered_copy(inverse, old_w))
    weight = lax.all_gather(own_w, "dp", axis=0, tiled=True)

    def meet(piece, by):
        groups = [[s, s ^ by] for s in range(sections) if s < s ^ by]
        return lax.all_gather(piece, "section", axis=0, tiled=False, axis_index_groups=groups)

    sources = section_index ^ layer_ids
    sides = (section_index < sources).astype(jnp.int32)
    picks = jnp.take(inverse, sources)
    early = picked_pieces(picks[:EARLY], old_v)
    received = [early[0]] + [meet(early[by], by) for by in range(1, EARLY)]
    picks_m = inverse + zero_after(own_w) + zero_after(received[-1])
    moment_one = relocate(ordered_copy(picks_m, old_m))
    late = picked_pieces(picks[EARLY:] + zero_after(own_w), old_v)
    received += [meet(late[by - EARLY], by) for by in range(EARLY, sections)]
    entry_section = section_index + zero_after(moment_one)
    weight = resident(weight)

    gain_row = norm_gain[0]

    def half_of(value, by=0):
        start = lax.rem(core_index + by, cores) * half_width
        return lax.dynamic_slice_in_dim(value, start, half_width, value.ndim - 1)

    def core_at(by):
        return lax.rem(core_index + by, cores).reshape(1)


    def put(stash, value, slot):
        return lax.dynamic_update_index_in_dim(stash, value, slot, 0)

    def get(stash, slot):
        return lax.dynamic_index_in_dim(stash, slot, 0, keepdims=False)

    def slot_of(group):
        return jnp.where((group >= 0) & (group < GROUPS), group, GROUPS)

    def hop(value, tick, by):
        senders = [tick - group for group in range(GROUPS) if 0 <= tick - group < sections - 1]
        pairs = [(s, s + 1) for s in senders]
        if by < 0:
            pairs = [(sections - 1 - s, sections - 2 - s) for s in senders]
        return lax.ppermute(value, "section", pairs)

    acts = jnp.zeros((GROUPS + 1, group_rows, full_width), jnp.bfloat16)
    norms = jnp.zeros((GROUPS + 1, group_rows, full_width), jnp.bfloat16)
    preacts = jnp.zeros((GROUPS + 1, group_rows, half_width), jnp.float32)
    slopes = jnp.zeros((GROUPS + 1, group_rows, half_width), jnp.float32)
    scales = jnp.zeros((GROUPS + 1, group_rows, 128), jnp.float32)
    dpres = jnp.zeros((GROUPS + 1, group_rows, half_width), jnp.bfloat16)
    ticks = GROUPS + sections - 1
    features = None
    forward_in = jnp.zeros((group_rows, full_width), jnp.bfloat16)
    backward_in = jnp.zeros((group_rows, half_width), jnp.bfloat16)

    def forward_tick(tick, arriving, stash, weight):
        acts, norms, preacts, slopes, scales = stash
        slot = slot_of(tick - section_index)
        inputs = arriving
        if tick < GROUPS:
            entry = tokens[tick * group_rows : (tick + 1) * group_rows]
            inputs = jnp.where(entry_section == 0, entry, arriving)
        output, normed, preact, scale, weight = forward_step(core_at(0), inputs, norm_gain, weight)
        sigmoid_value = jax.nn.sigmoid(preact)
        slope = sigmoid_value * (1.0 + preact * (1.0 - sigmoid_value))
        stash = (
            put(acts, inputs, slot),
            put(norms, normed, slot),
            put(preacts, preact, slot),
            put(slopes, slope, slot),
            put(scales, scale, slot),
        )
        if tick < ticks - 1:
            arriving = lax.all_gather(hop(output, tick, 1), "mp", axis=1, tiled=True)
        return arriving, stash, weight

    def backward_tick(tick, arriving, stash, dpres, weight):
        acts, _, preacts, slopes, scales = stash
        slot = slot_of(tick - (sections - 1 - section_index))
        slope, preact, inputs = get(slopes, slot), get(preacts, slot), get(acts, slot)
        row_scale = get(scales, slot)
        slope, preact, row_scale, inputs = lax.optimization_barrier(
            (slope, preact, row_scale, inputs)
        )
        upstream = arriving
        if tick < GROUPS:
            seed = cotangent[tick * group_rows : (tick + 1) * group_rows]
            upstream = jnp.where(section_index == sections - 1, half_of(seed), arriving)
        if tick == ticks - 1:
            dpre = (upstream.astype(jnp.float32) * slope).astype(jnp.bfloat16)
            return arriving, put(dpres, dpre, slot), weight
        for by in range(1, cores):
            dpre, stat, away, weight = backward_away(
                core_at(by), upstream, slope, preact, inputs, row_scale, norm_gain, weight
            )
            came = turn(away, "mp", by)
        home, weight = backward_home(
            core_at(0), upstream, dpre, stat, inputs, row_scale, norm_gain, weight
        )
        arriving = hop((home + came.astype(jnp.float32)).astype(jnp.bfloat16), tick, -1)
        return arriving, put(dpres, dpre, slot), weight

    stash = (acts, norms, preacts, slopes, scales)
    for tick in range(ticks - 1):
        forward_in, stash, weight = forward_tick(tick, forward_in, stash, weight)
    last_stash = stash
    for tick in range(ticks):
        if tick == 1:
            _, stash, weight = forward_tick(ticks - 1, forward_in, last_stash, weight)
        backward_in, dpres, weight = backward_tick(tick, backward_in, stash, dpres, weight)
        if tick == GROUPS:
            block_start = replica_index
            normed_all = stash[1][:GROUPS].reshape(token_total, full_width)
            features = []
            for by in range(replicas):
                block = lax.rem(block_start + by, replicas) * row_block
                part = lax.dynamic_slice_in_dim(normed_all, block, row_block, 1)
                features.append(turn(part, "dp", by) if by else part)
            features = jnp.concatenate(features, axis=0)
            features = features.T.reshape(sections, -1, replicas * token_total)

    dpre_all = dpres[:GROUPS].reshape(token_total, half_width)
    dpre_all = jnp.concatenate(
        [turn(dpre_all, "dp", by) if by else dpre_all for by in range(replicas)], axis=0
    )
    blocked = (sections, -1, half_width)
    updated = adam(
        sources,
        sides,
        features,
        dpre_all,
        own_w.reshape(blocked),
        moment_one.reshape(blocked),
        received,
    )
    return tuple(value.reshape(1, row_block, half_width) for value in updated)


def solution(mesh):
    placed = (
        P(None, "dp", "section", None, "mp"),
        P(None, "dp", "section", None, "mp"),
        P(None, "dp", "section", None, "mp"),
        P(),
        P("section", None),
        P(None, "dp", None),
        P(None, "dp", None),
    )
    return jax.shard_map(
        local,
        mesh=mesh,
        in_specs=placed,
        out_specs=(P("section", "dp", "mp"), P("section", "dp", "mp"), P("section", "dp", "mp")),
        check_vma=False,
    )
```

time: 713 us -> 608 us (0.85)
  blocking collectives: 82.6 us -> 17.2 us
  matrix products: 60.8 us -> 0 us
  Pallas kernels: 23.1 us -> 79.9 us
  other arithmetic: 40.2 us -> 3.24 us
  waiting for transfers between devices: 409 us -> 418 us
    all_gather x2 -> x8, waiting for transfers between devices: 78.5 us -> 0.15 us  [the longest x7 0.13 us: meet(): lax.all_gather(piece, 'section', axis=0, tiled=False, axis_index_groups=g...]
    all_to_all x1 -> x0, blocking collectives: 65.3 us -> none  [relocate(): lax.all_to_all(pieces, 'section', split_axis=0, concat_axis=2, tiled=True)]
    ppermute x16, waiting for transfers between devices: 116 us -> 178 us  [hop(): return lax.ppermute(value, 'section', pairs)]
    dot_general x25 -> x0, matrix products: 60.8 us -> none  [the longest x16 37.4 us: local(): jnp.dot(dpre, turned[by], preferred_element_type=jnp.float32)]
    pallas_call x2 -> x31, Pallas kernels: 23.1 us -> 79.9 us  [the longest x9 20.7 us: forward_step(): pl.pallas_call(body, in_specs=[SCALAR, WHOLE, WHOLE, WHOLE], out_specs=[W...]
    all_to_all x3 -> x2, waiting for transfers between devices: 197 us -> 227 us  [relocate(): lax.all_to_all(pieces, 'section', split_axis=0, concat_axis=2, tiled=True)]
    unnamed x106 -> x20, local copies, waits for them, and re-layouts: 4.37 us -> 19.8 us
    gather x2 -> x1, local copies, waits for them, and re-layouts: 13.4 us -> 0.64 us  [local(): picks = jnp.take(inverse, sources)]
  transfers between devices with their start and end apart: 31 -> 36, of which waited for: 17 -> 8; matrix products, arithmetic and copies ran while one was open for 7% -> 2% of each run, Pallas kernels for 0% -> 10%
where the time goes in v2:
time: 608 us; the launch traced here: 600 us
  waiting for transfers between devices  418 us (69%)
  Pallas kernels  79.9 us (13%)
  starting transfers between devices  35.9 us (6%)
  local copies, waits for them, and re-layouts  27 us (4%)
  between operations  17.9 us (3%)
  blocking collectives  17.2 us (3%)
    all_to_all x2, waiting for transfers between devices, relocate(): lax.all_to_all(pieces, 'section', split_axis=0, concat_axis=2, tiled=True)  227 us
    ppermute x16, waiting for transfers between devices, hop(): return lax.ppermute(value, 'section', pairs)  178 us
    pallas_call x9, Pallas kernels, forward_step(): pl.pallas_call(body, in_specs=[SCALAR, WHOLE, WHOLE, WHOLE], out_specs=[W...  20.7 us
    pallas_call x1, Pallas kernels, adam(): pl.pallas_call(body, grid_spec=pltpu.PrefetchScalarGridSpec(num_scalar_pr...  20.1 us
    unnamed x20, local copies, waits for them, and re-layouts  19.8 us
    ppermute x16, starting transfers between devices, hop(): return lax.ppermute(value, 'section', pairs)  18.7 us
    all_gather x8, blocking collectives, forward_tick(): arriving = lax.all_gather(hop(output, tick, 1), 'mp', axis=1, tiled=True)  17.2 us
    pallas_call x8, Pallas kernels, backward_away(): pl.pallas_call(body, in_specs=[SCALAR] + [WHOLE] * 7, out_specs=[WHOLE] *...  14.3 us
  transfers between devices with their start and end apart: 36, of which 8 were waited for; matrix products, arithmetic and copies ran while one was open for 2% of the time, Pallas kernels for 10%

profile of v2, /device:TPU:0, one launch (start us, length us, event | category | flops | bytes accessed | tf_op | source)
XLA Modules:
  0.0 599.6 jit_solution(4364228857467864999)
XLA Ops:
  7.9 4.1 copy-done.4
  13.3 2.4 copy-done
  15.8 7.3 %all-to-all-start = ((bf16[8,1,1,208,1664]{4,3,2,1,0:T(8,128)(2,1)}), bf16[8,1,1,208,1664]{4,3,2,1,0:T(8,128)(2,1)}, u32[]{:S(2)}, u32[]{:S(2)}) async-start(bf16[8,1,1,208,1664]{4,3,2,1,0:T(8,128)(2,1)} %copy-done), calls=%async_computation | async-start | bytes 11075584 | tf_op jit(solution)/shard_map/all_to_all | solution.py:33
  23.8 2.6 copy-done.1
  29.0 116.2 %all-to-all-done = bf16[8,1,1,208,1664]{4,3,2,1,0:T(8,128)(2,1)} async-done(((bf16[8,1,1,208,1664]{4,3,2,1,0:T(8,128)(2,1)}), bf16[8,1,1,208,1664]{4,3,2,1,0:T(8,128)(2,1)}, u32[]{:S(2)}, u32[]{:S(2)}) %all-to-all-start) | async-done | bytes 5537824 | tf_op jit(solution)/shard_map/all_to_all | solution.py:33
  148.9 3.3 copy-done.6
  153.3 3.3 copy-done.3
  156.6 4.7 all-to-all-start.1
  161.4 3.1 copy-done.2
  164.6 2.6 shard_map.123
  170.4 111.2 %all-to-all-done.1 = bf16[8,1,1,208,1664]{4,3,2,1,0:T(8,128)(2,1)} async-done(((bf16[8,1,1,208,1664]{4,3,2,1,0:T(8,128)(2,1)}), bf16[8,1,1,208,1664]{4,3,2,1,0:T(8,128)(2,1)}, u32[]{:S(2)}, u32[]{:S(2)}) %all-to-all-start.1) | async-done | bytes 5537824 | tf_op jit(solution)/shard_map/all_to_all | solution.py:33
  283.7 4.2 shard_map.97.w_ref
  287.9 2.2 shard_map.98
  290.1 3.4 collective-permute-start
  294.1 3.1 collective-permute-done
  299.5 2.2 shard_map.99
  301.7 4.4 collective-permute-start.1
  306.4 4.5 collective-permute-done.1
  313.0 2.2 shard_map.100
  316.2 2.1 all_gather.74.x_ref
  318.3 2.2 shard_map.101
  321.5 2.3 all_gather.75.x_ref
  323.8 2.2 shard_map.102
  329.1 2.2 shard_map.103
  334.4 2.2 shard_map.104
  339.6 2.2 shard_map.105
  342.9 2.3 all_gather.79.x_ref
  348.9 2.9 shard_map.108
  384.6 160.4 %collective-permute-done.22.up_ref = bf16[64,1664]{1,0:T(8,128)(2,1)S(1)} collective-permute-done((bf16[64,1664]{1,0:T(8,128)(2,1)S(1)}, bf16[64,1664]{1,0:T(8,128)(2,1)S(1)}, u32[]{:S(2)}, u32[]{:S(2)}) %collective-permute-start.22) | collective-permute-done | bytes 213024 | tf_op jit(solution)/shard_map/ppermute | solution.py:372
  550.1 10.2 %collective-permute-done.24 = bf16[64,1664]{1,0:T(8,128)(2,1)S(1)} collective-permute-done((bf16[64,1664]{1,0:T(8,128)(2,1)S(1)}, bf16[64,1664]{1,0:T(8,128)(2,1)S(1)}, u32[]{:S(2)}, u32[]{:S(2)}) %collective-permute-start.24) | collective-permute-done | bytes 213024 | tf_op jit(solution)/shard_map/ppermute | solution.py:372
  562.5 9.5 %collective-permute-done.25 = bf16[128,1664]{1,0:T(8,128)(2,1)S(1)} collective-permute-done((bf16[128,1664]{1,0:T(8,128)(2,1)S(1)}, bf16[128,1664]{1,0:T(8,128)(2,1)S(1)}, u32[]{:S(2)}, u32[]{:S(2)}) %collective-permute-start.25) | collective-permute-done | bytes 426016 | tf_op jit(solution)/shard_map/ppermute | solution.py:24
  572.2 20.1 %shard_map.124 = (f32[8,208,1664]{2,1,0:T(8,128)}, bf16[8,208,1664]{2,1,0:T(8,128)(2,1)}, bf16[8,208,1664]{2,1,0:T(8,128)(2,1)}) custom-call(s32[8]{0:T(128)S(1)} %iota_xor_fusion.order_ref, s32[8]{0:T(128)S(1)} %compare_convert_fusion.side_ref, bf16[8,208,256]{2,1,0:T(8,128)(2,1)S(1)} %bitcast.211, bf16[256,1664]{1,0:T(8,128)(2,1)S(1)} %pad_maximum_fusion.dpre_ref, ...), custom_call_target="tpu_custom_call" | custom-call | tf_op jit(solution)/shard_map/pallas_call | solution.py:276
  (194 shorter events, 73.7 us)
Async XLA Ops:
  15.8 129.4 %all-to-all-start = ((bf16[8,1,1,208,1664]{4,3,2,1,0:T(8,128)(2,1)}), bf16[8,1,1,208,1664]{4,3,2,1,0:T(8,128)(2,1)}, u32[]{:S(2)}, u32[]{:S(2)}) async-start(bf16[8,1,1,208,1664]{4,3,2,1,0:T(8,128)(2,1)} %copy-done), calls=%async_computation | async-start | bytes 11075584 | tf_op jit(solution)/shard_map/all_to_all | solution.py:33
  23.1 122.1 %all-gather.18.cloned.1.call-start = ((), (), s32[]{:S(2)}) async-start(), calls=%async_computation.3 | async-start | bytes 2076672 | tf_op jit(solution)/shard_map/all_gather | solution.py:334
  28.9 254.8 %all-gather.16.cloned.1.call-start = ((), (), s32[]{:S(2)}) async-start(), calls=%async_computation.2 | async-start | bytes 16613376 | tf_op jit(solution)/shard_map/all_gather | solution.py:330
  156.6 125.0 %all-to-all-start.1 = ((bf16[8,1,1,208,1664]{4,3,2,1,0:T(8,128)(2,1)}), bf16[8,1,1,208,1664]{4,3,2,1,0:T(8,128)(2,1)}, u32[]{:S(2)}, u32[]{:S(2)}) async-start(bf16[8,1,1,208,1664]{4,3,2,1,0:T(8,128)(2,1)} %copy-done.3), calls=%async_computation.1 | async-start | bytes 11075584 | tf_op jit(solution)/shard_map/all_to_all | solution.py:33
  161.3 410.8 %all-gather.20.cloned.1.call-start = ((), (), s32[]{:S(2)}) async-start(), calls=%async_computation.4 | async-start | bytes 2076672 | tf_op jit(solution)/shard_map/all_gather | solution.py:334
  167.2 404.9 %all-gather.22.cloned.1.call-start = ((), (), s32[]{:S(2)}) async-start(), calls=%async_computation.5 | async-start | bytes 2076672 | tf_op jit(solution)/shard_map/all_gather | solution.py:334
  167.8 404.4 %all-gather.24.cloned.1.call-start = ((), (), s32[]{:S(2)}) async-start(), calls=%async_computation.6 | async-start | bytes 2076672 | tf_op jit(solution)/shard_map/all_gather | solution.py:334
  168.4 403.8 %all-gather.26.cloned.1.call-start = ((), (), s32[]{:S(2)}) async-start(), calls=%async_computation.7 | async-start | bytes 2076672 | tf_op jit(solution)/shard_map/all_gather | solution.py:334
  168.9 403.3 %all-gather.28.cloned.1.call-start = ((), (), s32[]{:S(2)}) async-start(), calls=%async_computation.8 | async-start | bytes 2076672 | tf_op jit(solution)/shard_map/all_gather | solution.py:334
  169.7 402.5 %all-gather.30.cloned.1.call-start = ((), (), s32[]{:S(2)}) async-start(), calls=%async_computation.9 | async-start | bytes 2076672 | tf_op jit(solution)/shard_map/all_gather | solution.py:334
  290.1 7.1 %collective-permute-start = (bf16[64,1664]{1,0:T(8,128)(2,1)S(1)}, bf16[64,1664]{1,0:T(8,128)(2,1)S(1)}, u32[]{:S(2)}, u32[]{:S(2)}) collective-permute-start(bf16[64,1664]{1,0:T(8,128)(2,1)S(1)} %get-tuple-element.139), channel_id=1, source_target_pairs={{0,4},{1,5},{2,6},{3,7}} | collective-permute-start | bytes 638984 | tf_op jit(solution)/shard_map/ppermute | solution.py:372
  301.7 9.2 %collective-permute-start.1 = (bf16[64,1664]{1,0:T(8,128)(2,1)S(1)}, bf16[64,1664]{1,0:T(8,128)(2,1)S(1)}, u32[]{:S(2)}, u32[]{:S(2)}) collective-permute-start(bf16[64,1664]{1,0:T(8,128)(2,1)S(1)} %get-tuple-element.142), channel_id=1, source_target_pairs={{4,8},{0,4},{5,9},{1,5},{6,10},{2,6},{7,11},{3,7}} | collective-permute-start | bytes 638984 | tf_op jit(solution)/shard_map/ppermute | solution.py:372
  315.2 1.0 collective-permute-start.2
  320.5 1.0 collective-permute-start.3
  326.0 0.9 collective-permute-start.4
  331.3 0.9 collective-permute-start.5
  336.6 0.9 collective-permute-start.6
  341.9 1.0 collective-permute-start.7
  351.8 1.5 collective-permute-start.9
  353.3 0.7 collective-permute-start.10
  355.9 2.0 collective-permute-start.11
  360.5 2.2 collective-permute-start.13
  365.3 2.1 collective-permute-start.15
  367.4 2.6 collective-permute-start.16
  368.4 193.4 %collective-permute-start.8 = (bf16[128,1664]{1,0:T(8,128)(2,1)S(1)}, bf16[128,1664]{1,0:T(8,128)(2,1)S(1)}, u32[]{:S(2)}, u32[]{:S(2)}) collective-permute-start(bf16[128,1664]{1,0:T(8,128)(2,1)S(1)} %get-tuple-element.298), channel_id=1, source_target_pairs={{0,2},{2,0},{1,3},{3,1},{4,6},{6,4},{5,7},{7,5},{8,10},{10,8},{9,1... | collective-permute-start | bytes 1277960 | tf_op jit(solution)/shard_map/ppermute | solution.py:24
  371.8 2.0 collective-permute-start.17
  376.4 2.3 collective-permute-start.19
  381.3 1.9 collective-permute-start.21
  383.2 161.8 %collective-permute-start.22 = (bf16[64,1664]{1,0:T(8,128)(2,1)S(1)}, bf16[64,1664]{1,0:T(8,128)(2,1)S(1)}, u32[]{:S(2)}, u32[]{:S(2)}) collective-permute-start(bf16[64,1664]{1,0:T(8,128)(2,1)S(1)} %add_convert_fusion.1), channel_id=1, source_target_pairs={{4,0},{8,4},{5,1},{9,5},{6,2},{10,6},{7,3},{11,7}} | collective-permute-start | bytes 638984 | tf_op jit(solution)/shard_map/ppermute | solution.py:372
  546.8 1.9 collective-permute-start.23
  548.7 11.5 %collective-permute-start.24 = (bf16[64,1664]{1,0:T(8,128)(2,1)S(1)}, bf16[64,1664]{1,0:T(8,128)(2,1)S(1)}, u32[]{:S(2)}, u32[]{:S(2)}) collective-permute-start(bf16[64,1664]{1,0:T(8,128)(2,1)S(1)} %add_convert_fusion), channel_id=1, source_target_pairs={{4,0},{5,1},{6,2},{7,3}} | collective-permute-start | bytes 638984 | tf_op jit(solution)/shard_map/ppermute | solution.py:372
  560.3 11.7 %collective-permute-start.25 = (bf16[128,1664]{1,0:T(8,128)(2,1)S(1)}, bf16[128,1664]{1,0:T(8,128)(2,1)S(1)}, u32[]{:S(2)}, u32[]{:S(2)}) collective-permute-start(bf16[128,1664]{1,0:T(8,128)(2,1)S(1)} %bitcast.214), channel_id=1, source_target_pairs={{0,2},{2,0},{1,3},{3,1},{4,6},{6,4},{5,7},{7,5},{8,10},{10,8},{9,1... | collective-permute-start | bytes 1277960 | tf_op jit(solution)/shard_map/ppermute | solution.py:24
  (14 other events, 142.6 us)
Sparse Core Ops, SparseCore 0:
  29.0 54.8 all-gather.17
  145.3 135.0 all-gather.15
  282.5 25.0 all-gather.19
  309.6 25.9 all-gather.21
  337.1 42.6 all-gather.23
  381.1 44.9 all-gather.25
  427.7 25.2 all-gather.27
  454.5 39.9 all-gather.29

commit v3 on v2

--- a/solution.py
+++ b/solution.py
@@ -14,9 +14,11 @@
 step_count = 1000.0
 
 GROUPS = 2
-EARLY = 2
+
+FIRST_PART = 8
+PARTS = 2
 STEP_VMEM = 16 * 1024 * 1024
-ADAM_VMEM = 20 * 1024 * 1024
+ADAM_VMEM = 24 * 1024 * 1024
 
 
 def turn(value, axis, by):
@@ -34,51 +36,117 @@
     return moved.reshape(-1, moved.shape[-1])
 
 
-def ordered_copy(picks, pieces):
+def ordered_cast(picks, pieces, cuts):
     slots, _, _, rows, width = pieces.shape
 
-    def body(pick_ref, in_ref, out_ref):
-        out_ref[...] = in_ref[...].astype(out_ref.dtype)
+    def body(pick_ref, in_ref, *out_refs):
+        for (lo, hi), out_ref in zip(cuts, out_refs):
+            out_ref[...] = in_ref[:, :, :, :, lo:hi].astype(out_ref.dtype)
 
     return pl.pallas_call(
         body,
-        out_shape=jax.ShapeDtypeStruct((picks.shape[0], 1, 1, rows, width), jnp.bfloat16),
+        out_shape=[
+            jax.ShapeDtypeStruct((slots, 1, 1, rows, hi - lo), jnp.bfloat16) for lo, hi in cuts
+        ],
         grid_spec=pltpu.PrefetchScalarGridSpec(
             num_scalar_prefetch=1,
-            grid=(picks.shape[0],),
+            grid=(slots,),
             in_specs=[pl.BlockSpec((1, 1, 1, rows, width), lambda i, p: (p[i], 0, 0, 0, 0))],
-            out_specs=pl.BlockSpec((1, 1, 1, rows, width), lambda i, p: (i, 0, 0, 0, 0)),
+            out_specs=[
+                pl.BlockSpec((1, 1, 1, rows, hi - lo), lambda i, p: (i, 0, 0, 0, 0))
+                for lo, hi in cuts
+            ],
         ),
         compiler_params=pltpu.CompilerParams(vmem_limit_bytes=STEP_VMEM),
     )(picks, pieces)
 
 
-def resident(array):
-    def body(in_ref, out_ref, sem):
-        copy = pltpu.make_async_copy(in_ref, out_ref, sem)
-        copy.start()
-        copy.wait()
-
-    return pl.pallas_call(
-        body,
-        out_shape=pltpu.VMEM(array.shape, array.dtype),
-        in_specs=[pl.BlockSpec(memory_space=pl.ANY)],
-        out_specs=pl.BlockSpec(memory_space=pltpu.VMEM),
-        scratch_shapes=[pltpu.SemaphoreType.DMA],
-        compiler_params=pltpu.CompilerParams(vmem_limit_bytes=STEP_VMEM),
-    )(in_hbm(array))
-
-
-def picked_pieces(picks, pieces):
-    _, _, _, rows, width = pieces.shape
+def picked(picks, carry, sources, edges, stacked):
+    rows = sources[0][0].shape[3]
     count = picks.shape[0]
-
-    def body(pick_ref, in_ref, *refs):
-        out_refs, sems = refs[:count], refs[count]
-        copies = [
-            pltpu.make_async_copy(in_ref.at[pick_ref[i], 0, 0], out_refs[i], sems.at[i])
+    ends = [0]
+    for _, lo, hi in sources:
+        ends.append(ends[-1] + hi - lo)
+    dtype = sources[0][0].dtype
+    spans = list(zip(edges[:-1], edges[1:]))
+
+    def body(pick_ref, carry_ref, *refs):
+        in_refs, refs = refs[: len(sources)], refs[len(sources) :]
+        carried_ref, out_refs, (held_ref, sems, out_sems) = refs[0], refs[1:-3], refs[-3:]
+        incoming = [
+            [
+                pltpu.make_async_copy(
+                    in_ref.at[pick_ref[i], 0, 0, :, lo:hi],
+                    held_ref.at[i, :, ends[j] : ends[j + 1]],
+                    sems.at[i, j],
+                )
+                for j, (in_ref, (_, lo, hi)) in enumerate(zip(in_refs, sources))
+            ]
             for i in range(count)
         ]
+        outgoing = [
+            [
+                pltpu.make_async_copy(
+                    held_ref.at[i, :, lo:hi],
+                    out_refs[0].at[i, 0, 0] if stacked else out_refs[i * len(spans) + j],
+                    out_sems.at[i, j],
+                )
+                for j, (lo, hi) in enumerate(spans)
+            ]
+            for i in range(count)
+        ]
+        for copies in incoming:
+            for copy in copies:
+                copy.start()
+        for i in range(carry_ref.shape[0]):
+            carried_ref[i] = carry_ref[i]
+        for arrive, leave in zip(incoming, outgoing):
+            for copy in arrive:
+                copy.wait()
+            for copy in leave:
+                copy.start()
+        for copies in outgoing:
+            for copy in copies:
+                copy.wait()
+
+    if stacked:
+        shapes = [jax.ShapeDtypeStruct((count, 1, 1, rows, ends[-1]), dtype)]
+    else:
+        shapes = [jax.ShapeDtypeStruct((rows, hi - lo), dtype) for lo, hi in spans] * count
+    carried, *pieces = pl.pallas_call(
+        body,
+        out_shape=[jax.ShapeDtypeStruct(carry.shape, carry.dtype)] + shapes,
+        in_specs=[SCALAR, SCALAR] + [ANYWHERE] * len(sources),
+        out_specs=[SCALAR] + [ANYWHERE] * len(shapes),
+        scratch_shapes=[
+            pltpu.VMEM((count, rows, ends[-1]), dtype),
+            pltpu.SemaphoreType.DMA((count, len(sources))),
+            pltpu.SemaphoreType.DMA((count, len(spans))),
+        ],
+        compiler_params=pltpu.CompilerParams(vmem_limit_bytes=STEP_VMEM),
+    )(picks, carry, *[in_hbm(array) for array, _, _ in sources])
+    if stacked:
+        return carried, pieces[0]
+    return carried, [pieces[i * len(spans) : (i + 1) * len(spans)] for i in range(count)]
+
+
+def resident(replica, blocks, cuts):
+    replicas = len(blocks)
+    rows = blocks[0][0].shape[0]
+    flat = [piece for line in blocks for piece in line]
+
+    def body(replica_ref, *refs):
+        piece_refs, out_ref, sems = refs[:-2], refs[-2], refs[-1]
+        copies = []
+        for index, piece_ref in enumerate(piece_refs):
+            by, (lo, hi) = index // len(cuts), cuts[index % len(cuts)]
+            owner = lax.rem(replica_ref[0] + replicas - by, replicas)
+            start = pl.multiple_of(owner * rows, 16)
+            copies.append(
+                pltpu.make_async_copy(
+                    piece_ref, out_ref.at[pl.ds(start, rows), lo:hi], sems.at[index]
+                )
+            )
         for copy in copies:
             copy.start()
         for copy in copies:
@@ -86,12 +154,12 @@
 
     return pl.pallas_call(
         body,
-        out_shape=[jax.ShapeDtypeStruct((rows, width), pieces.dtype)] * count,
-        in_specs=[pl.BlockSpec(memory_space=pltpu.SMEM), pl.BlockSpec(memory_space=pl.ANY)],
-        out_specs=[pl.BlockSpec(memory_space=pl.ANY)] * count,
-        scratch_shapes=[pltpu.SemaphoreType.DMA((count,))],
+        out_shape=pltpu.VMEM((replicas * rows, cuts[-1][1]), flat[0].dtype),
+        in_specs=[SCALAR] + [ANYWHERE] * len(flat),
+        out_specs=pl.BlockSpec(memory_space=pltpu.VMEM),
+        scratch_shapes=[pltpu.SemaphoreType.DMA((len(flat),))],
         compiler_params=pltpu.CompilerParams(vmem_limit_bytes=STEP_VMEM),
-    )(picks, pieces)
+    )(replica, *[in_hbm(piece) for piece in flat])
 
 
 def tiles_of(width):
@@ -218,53 +286,75 @@
     )(core, upstream, dpre, stat, inputs, row_scale, gain, in_vmem(weight))
 
 
-def adam(row_order, sides, features, dpre, master, moment_one, moment_two):
-    blocks, rows, width = moment_one.shape
-    depth = dpre.shape[0]
+def adam(row_order, sides, features, dpre, masters, moment_one, moments, cuts):
+    blocks, rows, first_width = moment_one.shape
+    depth, width = dpre.shape
+    parts = len(moments[0])
     strip = 16 if rows % 16 == 0 else rows
     fix_one = 1.0 - beta_one**step_count
     fix_two = 1.0 - beta_two**step_count
 
-    def body(order_ref, side_ref, feature_ref, dpre_ref, w_ref, m_ref, *refs):
-        second_refs, refs = refs[:blocks], refs[blocks:]
-        new_w_ref, new_m_ref, new_v_ref, grad_ref, v_ref, sems = refs
+    def body(order_ref, side_ref, feature_ref, dpre_ref, *refs):
+        w_refs, m_ref, refs = refs[: len(cuts)], refs[len(cuts)], refs[len(cuts) + 1 :]
+        piece_refs, refs = refs[: blocks * parts], refs[blocks * parts :]
+        new_w_ref, new_m_ref, new_v_ref, grad_ref, held_ref, sems = refs
         block = pl.program_id(0)
 
         def fetch(k):
-            source = second_refs[k].at[side_ref[k]] if k else second_refs[k]
-            return pltpu.make_async_copy(source, v_ref.at[k % 2], sems.at[k % 2])
+            copies, start = [], 0
+            for which in range(parts):
+                piece = piece_refs[parts * k + which]
+                piece = piece.at[side_ref[k]] if k else piece
+                end = start + piece.shape[-1]
+                copies.append(
+                    pltpu.make_async_copy(
+                        piece, held_ref.at[k % 2, :, start:end], sems.at[which, k % 2]
+                    )
+                )
+                start = end
+            return copies
 
         @pl.when(block == 0)
         def _():
-            fetch(0).start()
+            for copy in fetch(0):
+                copy.start()
 
         for k in range(blocks):
 
             @pl.when(block == k)
             def _(k=k):
                 if k + 1 < blocks:
-                    fetch(k + 1).start()
-                fetch(k).wait()
+                    for copy in fetch(k + 1):
+                        copy.start()
+
+        grad_ref[...] = jnp.dot(feature_ref[0], dpre_ref[...], preferred_element_type=jnp.float32)
+
+        for k in range(blocks):
+
+            @pl.when(block == k)
+            def _(k=k):
+                for copy in fetch(k):
+                    copy.wait()
 
         now = lax.rem(block, 2)
-        grad_ref[...] = jnp.dot(
-            feature_ref[0], dpre_ref[...], preferred_element_type=jnp.float32
-        )
 
         def step(index, carry):
             part = pl.ds(index * strip, strip)
-            grad = grad_ref[part, :]
-            moment_next = beta_one * m_ref[0, part, :].astype(jnp.float32) + (1.0 - beta_one) * grad
-            second_next = (
-                beta_two * v_ref[now, part, :].astype(jnp.float32) + (1.0 - beta_two) * grad * grad
-            )
-            scaled = second_next / fix_two
-            root = scaled * lax.rsqrt(scaled)
-            direction = moment_next / fix_one * pl.reciprocal(root + adam_eps, approx=True)
-            rows_w = w_ref[0, part, :].astype(jnp.float32)
-            new_w_ref[0, part, :] = rows_w - learn_rate * (direction + decay_rate * rows_w)
-            new_m_ref[0, part, :] = moment_next.astype(jnp.bfloat16)
-            new_v_ref[0, part, :] = second_next.astype(jnp.bfloat16)
+            for which, (lo, hi) in enumerate(cuts):
+                grad = grad_ref[part, lo:hi]
+                first = held_ref[now, part, width:] if which else m_ref[0, part, :]
+                moment_next = beta_one * first.astype(jnp.float32) + (1.0 - beta_one) * grad
+                second_next = (
+                    beta_two * held_ref[now, part, lo:hi].astype(jnp.float32)
+                    + (1.0 - beta_two) * grad * grad
+                )
+                scaled = second_next / fix_two
+                root = scaled * lax.rsqrt(scaled)
+                direction = moment_next / fix_one * pl.reciprocal(root + adam_eps, approx=True)
+                rows_w = w_refs[which][0, part, :].astype(jnp.float32)
+                new_w_ref[0, part, lo:hi] = rows_w - learn_rate * (direction + decay_rate * rows_w)
+                new_m_ref[0, part, lo:hi] = moment_next.astype(jnp.bfloat16)
+                new_v_ref[0, part, lo:hi] = second_next.astype(jnp.bfloat16)
             return carry
 
         lax.fori_loop(0, rows // strip, step, 0)
@@ -281,15 +371,15 @@
             in_specs=[
                 pl.BlockSpec((1, rows, depth), placed),
                 pl.BlockSpec((depth, width), lambda i, o, s: (0, 0)),
-                tile,
-                tile,
             ]
-            + [pl.BlockSpec(memory_space=pl.ANY)] * blocks,
+            + [pl.BlockSpec((1, rows, hi - lo), placed) for lo, hi in cuts]
+            + [pl.BlockSpec((1, rows, first_width), placed)]
+            + [ANYWHERE] * (blocks * parts),
             out_specs=[tile, tile, tile],
             scratch_shapes=[
                 pltpu.VMEM((rows, width), jnp.float32),
-                pltpu.VMEM((2, rows, width), jnp.bfloat16),
-                pltpu.SemaphoreType.DMA((2,)),
+                pltpu.VMEM((2, rows, 2 * width - first_width), jnp.bfloat16),
+                pltpu.SemaphoreType.DMA((parts, 2)),
             ],
         ),
         out_shape=[
@@ -303,9 +393,9 @@
         sides,
         features,
         dpre,
-        in_hbm(master),
+        *[in_hbm(piece) for piece in masters],
         in_hbm(moment_one),
-        *[in_hbm(piece) for piece in moment_two],
+        *[in_hbm(piece) for pieces in moments for piece in pieces],
     )
 
 
@@ -326,24 +416,35 @@
     layer_ids = jnp.arange(sections, dtype=jnp.int32)
     matches = (old_slot_layer[None, :] == layer_ids[:, None]).astype(jnp.int32)
     inverse = jnp.sum(matches * layer_ids[None, :], axis=1)
-    own_w = relocate(ordered_copy(inverse, old_w))
-    weight = lax.all_gather(own_w, "dp", axis=0, tiled=True)
+    lanes = half_width // 128
+    middle = lanes * FIRST_PART // 16 * 128
+    cuts = [(0, middle), (middle, half_width)]
+    sources = section_index ^ layer_ids
+    sides = (section_index < sources).astype(jnp.int32)
+    picks = jnp.take(inverse, sources)
+    early = sections // 2
+    breadth = 2 * half_width - middle
+    edges = [breadth // 128 * part // PARTS * 128 for part in range(PARTS)] + [breadth]
+    travelling = [(old_v, 0, half_width), (old_m, middle, half_width)]
+    carried, sent = picked(picks[:early], inverse, travelling, edges, False)
+    own_w = [relocate(piece) for piece in ordered_cast(carried, old_w, cuts)]
+    blocks = [
+        [turn(piece, "dp", by) if by else piece for piece in own_w] for by in range(replicas)
+    ]
 
     def meet(piece, by):
         groups = [[s, s ^ by] for s in range(sections) if s < s ^ by]
         return lax.all_gather(piece, "section", axis=0, tiled=False, axis_index_groups=groups)
 
-    sources = section_index ^ layer_ids
-    sides = (section_index < sources).astype(jnp.int32)
-    picks = jnp.take(inverse, sources)
-    early = picked_pieces(picks[:EARLY], old_v)
-    received = [early[0]] + [meet(early[by], by) for by in range(1, EARLY)]
-    picks_m = inverse + zero_after(own_w) + zero_after(received[-1])
-    moment_one = relocate(ordered_copy(picks_m, old_m))
-    late = picked_pieces(picks[EARLY:] + zero_after(own_w), old_v)
-    received += [meet(late[by - EARLY], by) for by in range(EARLY, sections)]
-    entry_section = section_index + zero_after(moment_one)
-    weight = resident(weight)
+    moments = [sent[0]] + [[meet(piece, by) for piece in sent[by]] for by in range(1, early)]
+    held = zero_after(blocks[-1][-1])
+    _, ordered_m = picked(inverse + held, inverse, [(old_m, 0, middle)], [0, middle], True)
+    moment_one = relocate(ordered_m)
+    later = picks[early:] + zero_after(own_w[-1])
+    _, sent = picked(later, inverse, travelling, edges, False)
+    moments += [[meet(piece, by) for piece in sent[by - early]] for by in range(early, sections)]
+    entry_section = section_index
+    weight = resident((replica_index + zero_after(moment_one)).reshape(1), blocks, cuts)
 
     gain_row = norm_gain[0]
 
@@ -437,6 +538,8 @@
         if tick == 1:
             _, stash, weight = forward_tick(ticks - 1, forward_in, last_stash, weight)
         backward_in, dpres, weight = backward_tick(tick, backward_in, stash, dpres, weight)
+        if tick == ticks - 2:
+            settled = dpres[: GROUPS - 1].reshape(-1, half_width)
         if tick == GROUPS:
             block_start = replica_index
             normed_all = stash[1][:GROUPS].reshape(token_total, full_width)
@@ -448,19 +551,20 @@
             features = jnp.concatenate(features, axis=0)
             features = features.T.reshape(sections, -1, replicas * token_total)
 
-    dpre_all = dpres[:GROUPS].reshape(token_total, half_width)
-    dpre_all = jnp.concatenate(
-        [turn(dpre_all, "dp", by) if by else dpre_all for by in range(replicas)], axis=0
-    )
-    blocked = (sections, -1, half_width)
+    gathered = []
+    for by in range(replicas):
+        for part in (settled, dpres[GROUPS - 1]):
+            gathered.append(turn(part, "dp", by) if by else part)
+    blocked = (sections, -1)
     updated = adam(
         sources,
         sides,
         features,
-        dpre_all,
-        own_w.reshape(blocked),
-        moment_one.reshape(blocked),
-        received,
+        jnp.concatenate(gathered, axis=0),
+        [piece.reshape(blocked + piece.shape[1:]) for piece in own_w],
+        moment_one.reshape(blocked + moment_one.shape[1:]),
+        moments,
+        cuts,
     )
     return tuple(value.reshape(1, row_block, half_width) for value in updated)
 

time: 608 us -> 577 us (0.949)
  waiting for transfers between devices: 418 us -> 381 us
  local copies, waits for them, and re-layouts: 27 us -> 12.6 us
  starting transfers between devices: 35.9 us -> 46.7 us
  Pallas kernels: 79.9 us -> 89.6 us
    all_to_all x2 -> x3, waiting for transfers between devices: 227 us -> 113 us  [relocate(): lax.all_to_all(pieces, 'section', split_axis=0, concat_axis=2, tiled=True)]
    ppermute x10 -> x13, waiting for transfers between devices: 9.88 us -> 73.8 us  [turn(): lax.ppermute(value, axis, [(i, (i + by) % count) for i in range(count)])]
    unnamed x20 -> x14, local copies, waits for them, and re-layouts: 19.8 us -> 6.11 us
    pallas_call x5, Pallas kernels: 10.7 us -> 21.7 us  [the longest x3 12.6 us: picked(): pl.pallas_call(body, out_shape=[jax.ShapeDtypeStruct(carry.shape, carry.d...]
    ppermute x16, waiting for transfers between devices: 178 us -> 188 us  [hop(): return lax.ppermute(value, 'section', pairs)]
    all_to_all x2 -> x3, starting transfers between devices: 12 us -> 17.4 us  [relocate(): lax.all_to_all(pieces, 'section', split_axis=0, concat_axis=2, tiled=True)]
  transfers between devices with their start and end apart: 36 -> 46, of which waited for: 8 -> 11; matrix products, arithmetic and copies ran while one was open for 2% -> 1% of each run, Pallas kernels for 10% -> 12%
where the time goes in v3:
time: 577 us; the launch traced here: 568 us
  waiting for transfers between devices  381 us (66%)
  Pallas kernels  89.6 us (16%)
  starting transfers between devices  46.7 us (8%)
  between operations  17.7 us (3%)
  blocking collectives  17.2 us (3%)
  local copies, waits for them, and re-layouts  12.6 us (2%)
    ppermute x16, waiting for transfers between devices, hop(): return lax.ppermute(value, 'section', pairs)  188 us
    all_to_all x3, waiting for transfers between devices, relocate(): lax.all_to_all(pieces, 'section', split_axis=0, concat_axis=2, tiled=True)  113 us
    ppermute x13, waiting for transfers between devices, turn(): lax.ppermute(value, axis, [(i, (i + by) % count) for i in range(count)])  73.8 us
    pallas_call x9, Pallas kernels, forward_step(): pl.pallas_call(body, in_specs=[SCALAR, WHOLE, WHOLE, WHOLE], out_specs=[W...  20.7 us
    ppermute x16, starting transfers between devices, hop(): return lax.ppermute(value, 'section', pairs)  20.1 us
    pallas_call x1, Pallas kernels, adam(): pl.pallas_call(body, grid_spec=pltpu.PrefetchScalarGridSpec(num_scalar_pr...  18.7 us
    all_to_all x3, starting transfers between devices, relocate(): lax.all_to_all(pieces, 'section', split_axis=0, concat_axis=2, tiled=True)  17.4 us
    all_gather x8, blocking collectives, forward_tick(): arriving = lax.all_gather(hop(output, tick, 1), 'mp', axis=1, tiled=True)  17.2 us
  transfers between devices with their start and end apart: 46, of which 11 were waited for; matrix products, arithmetic and copies ran while one was open for 1% of the time, Pallas kernels for 12%

profile of v3, /device:TPU:0, one launch (start us, length us, event | category | flops | bytes accessed | tf_op | source)
XLA Modules:
  0.0 568.1 jit_solution(3245707084698717651)
XLA Ops:
  8.7 4.5 shard_map.94
  14.8 4.1 copy-done
  18.9 4.4 shard_map.95
  23.4 7.3 %all-to-all-start = ((bf16[8,1,1,208,896]{4,3,2,1,0:T(8,128)(2,1)}), bf16[8,1,1,208,896]{4,3,2,1,0:T(8,128)(2,1)S(1)}, u32[]{:S(2)}, u32[]{:S(2)}) async-start(bf16[8,1,1,208,896]{4,3,2,1,0:T(8,128)(2,1)} %get-tuple-element.150), calls=%async_computation | async-start | bytes 5963776 | tf_op jit(solution)/shard_map/all_to_all | solution.py:35
  33.9 64.0 %all-to-all-done = bf16[8,1,1,208,896]{4,3,2,1,0:T(8,128)(2,1)S(1)} async-done(((bf16[8,1,1,208,896]{4,3,2,1,0:T(8,128)(2,1)}), bf16[8,1,1,208,896]{4,3,2,1,0:T(8,128)(2,1)S(1)}, u32[]{:S(2)}, u32[]{:S(2)}) %all-to-all-start) | async-done | bytes 2981920 | tf_op jit(solution)/shard_map/all_to_all | solution.py:35
  97.8 4.4 all-to-all-start.2
  103.6 4.5 shard_map.123
  111.1 62.7 %collective-permute-done.refs_3_ = bf16[1664,896]{1,0:T(8,128)(2,1)} collective-permute-done((bf16[1664,896]{1,0:T(8,128)(2,1)S(1)}, bf16[1664,896]{1,0:T(8,128)(2,1)}, u32[]{:S(2)}, u32[]{:S(2)}) %collective-permute-start) | collective-permute-done | bytes 2981920 | tf_op jit(solution)/shard_map/ppermute | solution.py:26
  175.7 3.6 shard_map.96
  179.3 5.7 %all-to-all-start.1 = ((bf16[8,1,1,208,768]{4,3,2,1,0:T(8,128)(2,1)}), bf16[8,1,1,208,768]{4,3,2,1,0:T(8,128)(2,1)}, u32[]{:S(2)}, u32[]{:S(2)}) async-start(bf16[8,1,1,208,768]{4,3,2,1,0:T(8,128)(2,1)} %get-tuple-element.151), calls=%async_computation.1 | async-start | bytes 5111808 | tf_op jit(solution)/shard_map/all_to_all | solution.py:35
  189.0 49.0 %all-to-all-done.1 = bf16[8,1,1,208,768]{4,3,2,1,0:T(8,128)(2,1)} async-done(((bf16[8,1,1,208,768]{4,3,2,1,0:T(8,128)(2,1)}), bf16[8,1,1,208,768]{4,3,2,1,0:T(8,128)(2,1)}, u32[]{:S(2)}, u32[]{:S(2)}) %all-to-all-start.1) | async-done | bytes 2555936 | tf_op jit(solution)/shard_map/all_to_all | solution.py:35
  241.4 4.7 shard_map.97.w_ref
  246.1 2.2 shard_map.98
  248.3 4.8 collective-permute-start.2
  253.6 6.9 %collective-permute-done.2 = bf16[64,1664]{1,0:T(8,128)(2,1)S(1)} collective-permute-done((bf16[64,1664]{1,0:T(8,128)(2,1)S(1)}, bf16[64,1664]{1,0:T(8,128)(2,1)S(1)}, u32[]{:S(2)}, u32[]{:S(2)}) %collective-permute-start.2) | collective-permute-done | bytes 213024 | tf_op jit(solution)/shard_map/ppermute | solution.py:473
  262.7 2.2 shard_map.99
  265.0 4.4 collective-permute-start.3
  269.6 4.5 collective-permute-done.3
  276.3 2.2 shard_map.100
  281.6 2.2 shard_map.101
  284.8 2.3 all_gather.111.x_ref
  287.1 2.2 shard_map.102
  292.3 2.2 shard_map.103
  297.6 2.2 shard_map.104
  302.9 2.2 shard_map.105
  306.2 2.3 all_gather.115.x_ref
  312.1 2.9 shard_map.108
  347.9 160.8 %collective-permute-done.24.up_ref = bf16[64,1664]{1,0:T(8,128)(2,1)S(1)} collective-permute-done((bf16[64,1664]{1,0:T(8,128)(2,1)S(1)}, bf16[64,1664]{1,0:T(8,128)(2,1)S(1)}, u32[]{:S(2)}, u32[]{:S(2)}) %collective-permute-start.24) | collective-permute-done | bytes 213024 | tf_op jit(solution)/shard_map/ppermute | solution.py:473
  513.7 16.3 %collective-permute-done.26 = bf16[64,1664]{1,0:T(8,128)(2,1)S(1)} collective-permute-done((bf16[64,1664]{1,0:T(8,128)(2,1)S(1)}, bf16[64,1664]{1,0:T(8,128)(2,1)S(1)}, u32[]{:S(2)}, u32[]{:S(2)}) %collective-permute-start.26) | collective-permute-done | bytes 213024 | tf_op jit(solution)/shard_map/ppermute | solution.py:473
  532.9 5.4 collective-permute-done.28
  538.3 3.7 collective-permute-done.27
  542.4 18.7 %shard_map.124 = (f32[8,208,1664]{2,1,0:T(8,128)}, bf16[8,208,1664]{2,1,0:T(8,128)(2,1)}, bf16[8,208,1664]{2,1,0:T(8,128)(2,1)}) custom-call(s32[8]{0:T(128)S(1)} %iota_xor_fusion.order_ref, s32[8]{0:T(128)S(1)} %compare_convert_fusion.side_ref, bf16[8,208,256]{2,1,0:T(8,128)(2,1)S(1)} %bitcast.224, bf16[256,1664]{1,0:T(8,128)(2,1)S(1)} %pad_maximum_fusion.dpre_ref, ...), custom_call_target="tpu_custom_call" | custom-call | tf_op jit(solution)/shard_map/pallas_call | solution.py:366
  (214 shorter events, 80.8 us)
Async XLA Ops:
  7.2 534.9 %all-gather.29.cloned.1.call-start = ((), (), s32[]{:S(2)}) async-start(), calls=%async_computation.3 | async-start | bytes 1597440 | tf_op jit(solution)/shard_map/all_gather | solution.py:437
  23.4 74.5 %all-to-all-start = ((bf16[8,1,1,208,896]{4,3,2,1,0:T(8,128)(2,1)}), bf16[8,1,1,208,896]{4,3,2,1,0:T(8,128)(2,1)S(1)}, u32[]{:S(2)}, u32[]{:S(2)}) async-start(bf16[8,1,1,208,896]{4,3,2,1,0:T(8,128)(2,1)} %get-tuple-element.150), calls=%async_computation | async-start | bytes 5963776 | tf_op jit(solution)/shard_map/all_to_all | solution.py:35
  30.6 511.4 %all-gather.31.cloned.1.call-start = ((), (), s32[]{:S(2)}) async-start(), calls=%async_computation.4 | async-start | bytes 1597440 | tf_op jit(solution)/shard_map/all_gather | solution.py:437
  31.4 510.7 %all-gather.33.cloned.1.call-start = ((), (), s32[]{:S(2)}) async-start(), calls=%async_computation.5 | async-start | bytes 1597440 | tf_op jit(solution)/shard_map/all_gather | solution.py:437
  32.1 510.0 %all-gather.35.cloned.1.call-start = ((), (), s32[]{:S(2)}) async-start(), calls=%async_computation.6 | async-start | bytes 1597440 | tf_op jit(solution)/shard_map/all_gather | solution.py:437
  32.7 509.5 %all-gather.37.cloned.1.call-start = ((), (), s32[]{:S(2)}) async-start(), calls=%async_computation.7 | async-start | bytes 1597440 | tf_op jit(solution)/shard_map/all_gather | solution.py:437
  33.3 508.9 %all-gather.39.cloned.1.call-start = ((), (), s32[]{:S(2)}) async-start(), calls=%async_computation.8 | async-start | bytes 1597440 | tf_op jit(solution)/shard_map/all_gather | solution.py:437
  97.8 81.5 %all-to-all-start.2 = ((bf16[8,1,1,208,768]{4,3,2,1,0:T(8,128)(2,1)}), bf16[8,1,1,208,768]{4,3,2,1,0:T(8,128)(2,1)}, u32[]{:S(2)}, u32[]{:S(2)}) async-start(bf16[8,1,1,208,768]{4,3,2,1,0:T(8,128)(2,1)} %get-tuple-element.152), calls=%async_computation.2 | async-start | bytes 5111808 | tf_op jit(solution)/shard_map/all_to_all | solution.py:35
  102.3 439.9 %all-gather.41.cloned.1.call-start = ((), (), s32[]{:S(2)}) async-start(), calls=%async_computation.9 | async-start | bytes 1597440 | tf_op jit(solution)/shard_map/all_gather | solution.py:437
  108.1 434.1 %all-gather.43.cloned.1.call-start = ((), (), s32[]{:S(2)}) async-start(), calls=%async_computation.10 | async-start | bytes 1597440 | tf_op jit(solution)/shard_map/all_gather | solution.py:437
  108.2 65.6 %collective-permute-start = (bf16[1664,896]{1,0:T(8,128)(2,1)S(1)}, bf16[1664,896]{1,0:T(8,128)(2,1)}, u32[]{:S(2)}, u32[]{:S(2)}) collective-permute-start(bf16[1664,896]{1,0:T(8,128)(2,1)S(1)} %bitcast.227), channel_id=1, source_target_pairs={{0,2},{2,0},{1,3},{3,1},{4,6},{6,4},{5,7},{7,5},{8,10},{10,8},{9,1... | collective-permute-start | bytes 8945672 | tf_op jit(solution)/shard_map/ppermute | solution.py:26
  109.8 432.5 %all-gather.45.cloned.1.call-start = ((), (), s32[]{:S(2)}) async-start(), calls=%async_computation.11 | async-start | bytes 1597440 | tf_op jit(solution)/shard_map/all_gather | solution.py:437
  110.5 431.8 %all-gather.47.cloned.1.call-start = ((), (), s32[]{:S(2)}) async-start(), calls=%async_computation.12 | async-start | bytes 1597440 | tf_op jit(solution)/shard_map/all_gather | solution.py:437
  179.3 58.7 %all-to-all-start.1 = ((bf16[8,1,1,208,768]{4,3,2,1,0:T(8,128)(2,1)}), bf16[8,1,1,208,768]{4,3,2,1,0:T(8,128)(2,1)}, u32[]{:S(2)}, u32[]{:S(2)}) async-start(bf16[8,1,1,208,768]{4,3,2,1,0:T(8,128)(2,1)} %get-tuple-element.151), calls=%async_computation.1 | async-start | bytes 5111808 | tf_op jit(solution)/shard_map/all_to_all | solution.py:35
  185.0 357.3 %all-gather.49.cloned.1.call-start = ((), (), s32[]{:S(2)}) async-start(), calls=%async_computation.13 | async-start | bytes 1597440 | tf_op jit(solution)/shard_map/all_gather | solution.py:437
  185.7 356.6 %all-gather.51.cloned.1.call-start = ((), (), s32[]{:S(2)}) async-start(), calls=%async_computation.14 | async-start | bytes 1597440 | tf_op jit(solution)/shard_map/all_gather | solution.py:437
  186.1 55.3 %collective-permute-start.1 = (bf16[1664,768]{1,0:T(8,128)(2,1)}, bf16[1664,768]{1,0:T(8,128)(2,1)}, u32[]{:S(2)}, u32[]{:S(2)}) collective-permute-start(bf16[1664,768]{1,0:T(8,128)(2,1)} %bitcast.8.refs_0_), channel_id=1, source_target_pairs={{0,2},{2,0},{1,3},{3,1},{4,6},{6,4},{5,7},{7,5},{8,10},{10,8},{9,1... | collective-permute-start | bytes 7667720 | tf_op jit(solution)/shard_map/ppermute | solution.py:26
  187.6 354.7 %all-gather.53.cloned.1.call-start = ((), (), s32[]{:S(2)}) async-start(), calls=%async_computation.15 | async-start | bytes 1597440 | tf_op jit(solution)/shard_map/all_gather | solution.py:437
  188.4 354.0 %all-gather.55.cloned.1.call-start = ((), (), s32[]{:S(2)}) async-start(), calls=%async_computation.16 | async-start | bytes 1597440 | tf_op jit(solution)/shard_map/all_gather | solution.py:437
  248.3 12.2 %collective-permute-start.2 = (bf16[64,1664]{1,0:T(8,128)(2,1)S(1)}, bf16[64,1664]{1,0:T(8,128)(2,1)S(1)}, u32[]{:S(2)}, u32[]{:S(2)}) collective-permute-start(bf16[64,1664]{1,0:T(8,128)(2,1)S(1)} %get-tuple-element.154), channel_id=1, source_target_pairs={{0,4},{1,5},{2,6},{3,7}} | collective-permute-start | bytes 638984 | tf_op jit(solution)/shard_map/ppermute | solution.py:473
  265.0 9.2 %collective-permute-start.3 = (bf16[64,1664]{1,0:T(8,128)(2,1)S(1)}, bf16[64,1664]{1,0:T(8,128)(2,1)S(1)}, u32[]{:S(2)}, u32[]{:S(2)}) collective-permute-start(bf16[64,1664]{1,0:T(8,128)(2,1)S(1)} %get-tuple-element.157), channel_id=1, source_target_pairs={{4,8},{0,4},{5,9},{1,5},{6,10},{2,6},{7,11},{3,7}} | collective-permute-start | bytes 638984 | tf_op jit(solution)/shard_map/ppermute | solution.py:473
  319.2 2.0 collective-permute-start.13
  323.8 2.2 collective-permute-start.15
  328.6 2.1 collective-permute-start.17
  330.7 2.6 collective-permute-start.18
  331.7 200.4 %collective-permute-start.10 = (bf16[128,1664]{1,0:T(8,128)(2,1)S(1)}, bf16[128,1664]{1,0:T(8,128)(2,1)S(1)}, u32[]{:S(2)}, u32[]{:S(2)}) collective-permute-start(bf16[128,1664]{1,0:T(8,128)(2,1)S(1)} %get-tuple-element.322), channel_id=1, source_target_pairs={{0,2},{2,0},{1,3},{3,1},{4,6},{6,4},{5,7},{7,5},{8,10},{10,8},{9,1... | collective-permute-start | bytes 1277960 | tf_op jit(solution)/shard_map/ppermute | solution.py:26
  335.1 2.0 collective-permute-start.19
  339.7 2.3 collective-permute-start.21
  346.5 162.1 %collective-permute-start.24 = (bf16[64,1664]{1,0:T(8,128)(2,1)S(1)}, bf16[64,1664]{1,0:T(8,128)(2,1)S(1)}, u32[]{:S(2)}, u32[]{:S(2)}) collective-permute-start(bf16[64,1664]{1,0:T(8,128)(2,1)S(1)} %add_convert_fusion.1), channel_id=1, source_target_pairs={{4,0},{8,4},{5,1},{9,5},{6,2},{10,6},{7,3},{11,7}} | collective-permute-start | bytes 638984 | tf_op jit(solution)/shard_map/ppermute | solution.py:473
  512.4 17.6 %collective-permute-start.26 = (bf16[64,1664]{1,0:T(8,128)(2,1)S(1)}, bf16[64,1664]{1,0:T(8,128)(2,1)S(1)}, u32[]{:S(2)}, u32[]{:S(2)}) collective-permute-start(bf16[64,1664]{1,0:T(8,128)(2,1)S(1)} %add_convert_fusion), channel_id=1, source_target_pairs={{4,0},{5,1},{6,2},{7,3}} | collective-permute-start | bytes 638984 | tf_op jit(solution)/shard_map/ppermute | solution.py:473
  530.1 8.2 %collective-permute-start.28 = (bf16[64,1664]{1,0:T(8,128)(2,1)S(1)}, bf16[64,1664]{1,0:T(8,128)(2,1)S(1)}, u32[]{:S(2)}, u32[]{:S(2)}) collective-permute-start(bf16[64,1664]{1,0:T(8,128)(2,1)S(1)} %slice_bitcast_fusion), channel_id=1, source_target_pairs={{0,2},{2,0},{1,3},{3,1},{4,6},{6,4},{5,7},{7,5},{8,10},{10,8},{9,1... | collective-permute-start | bytes 638984 | tf_op jit(solution)/shard_map/ppermute | solution.py:26
  531.6 10.3 %collective-permute-start.27 = (bf16[64,1664]{1,0:T(8,128)(2,1)S(1)}, bf16[64,1664]{1,0:T(8,128)(2,1)S(1)}, u32[]{:S(2)}, u32[]{:S(2)}) collective-permute-start(bf16[64,1664]{1,0:T(8,128)(2,1)S(1)} %get-tuple-element.325), channel_id=1, source_target_pairs={{0,2},{2,0},{1,3},{3,1},{4,6},{6,4},{5,7},{7,5},{8,10},{10,8},{9,1... | collective-permute-start | bytes 638984 | tf_op jit(solution)/shard_map/ppermute | solution.py:26
  (21 other events, 39.2 us)
Sparse Core Ops, SparseCore 0:
  14.9 44.4 all-gather.28
  60.9 26.5 all-gather.30
  89.0 63.0 all-gather.32
  153.5 20.9 all-gather.34
  175.8 59.4 all-gather.36
  236.7 21.2 all-gather.38
  259.6 32.9 all-gather.40
  294.1 32.8 all-gather.42
  328.5 36.1 all-gather.44
  366.1 32.9 all-gather.46
  400.6 26.1 all-gather.48
  428.2 27.3 all-gather.50
  457.2 34.9 all-gather.52
  493.7 32.0 all-gather.54

commit v4 on v3

--- a/solution.py
+++ b/solution.py
@@ -289,21 +289,22 @@
 def adam(row_order, sides, features, dpre, masters, moment_one, moments, cuts):
     blocks, rows, first_width = moment_one.shape
     depth, width = dpre.shape
-    parts = len(moments[0])
+    counts = [len(pieces) for pieces in moments]
+    parts, total = max(counts), sum(counts)
     strip = 16 if rows % 16 == 0 else rows
     fix_one = 1.0 - beta_one**step_count
     fix_two = 1.0 - beta_two**step_count
 
     def body(order_ref, side_ref, feature_ref, dpre_ref, *refs):
         w_refs, m_ref, refs = refs[: len(cuts)], refs[len(cuts)], refs[len(cuts) + 1 :]
-        piece_refs, refs = refs[: blocks * parts], refs[blocks * parts :]
+        piece_refs, refs = refs[:total], refs[total:]
         new_w_ref, new_m_ref, new_v_ref, grad_ref, held_ref, sems = refs
         block = pl.program_id(0)
 
         def fetch(k):
             copies, start = [], 0
-            for which in range(parts):
-                piece = piece_refs[parts * k + which]
+            for which in range(counts[k]):
+                piece = piece_refs[sum(counts[:k]) + which]
                 piece = piece.at[side_ref[k]] if k else piece
                 end = start + piece.shape[-1]
                 copies.append(
@@ -348,11 +349,13 @@
                     beta_two * held_ref[now, part, lo:hi].astype(jnp.float32)
                     + (1.0 - beta_two) * grad * grad
                 )
-                scaled = second_next / fix_two
+                scaled = second_next * (1.0 / fix_two)
                 root = scaled * lax.rsqrt(scaled)
-                direction = moment_next / fix_one * pl.reciprocal(root + adam_eps, approx=True)
+                direction = moment_next * pl.reciprocal(root + adam_eps, approx=True)
                 rows_w = w_refs[which][0, part, :].astype(jnp.float32)
-                new_w_ref[0, part, lo:hi] = rows_w - learn_rate * (direction + decay_rate * rows_w)
+                new_w_ref[0, part, lo:hi] = (
+                    rows_w * (1.0 - learn_rate * decay_rate) - (learn_rate / fix_one) * direction
+                )
                 new_m_ref[0, part, lo:hi] = moment_next.astype(jnp.bfloat16)
                 new_v_ref[0, part, lo:hi] = second_next.astype(jnp.bfloat16)
             return carry
@@ -374,7 +377,7 @@
             ]
             + [pl.BlockSpec((1, rows, hi - lo), placed) for lo, hi in cuts]
             + [pl.BlockSpec((1, rows, first_width), placed)]
-            + [ANYWHERE] * (blocks * parts),
+            + [ANYWHERE] * total,
             out_specs=[tile, tile, tile],
             scratch_shapes=[
                 pltpu.VMEM((rows, width), jnp.float32),
@@ -426,7 +429,7 @@
     breadth = 2 * half_width - middle
     edges = [breadth // 128 * part // PARTS * 128 for part in range(PARTS)] + [breadth]
     travelling = [(old_v, 0, half_width), (old_m, middle, half_width)]
-    carried, sent = picked(picks[:early], inverse, travelling, edges, False)
+    carried, sent = picked(picks[:early], inverse, travelling, [0, breadth], False)
     own_w = [relocate(piece) for piece in ordered_cast(carried, old_w, cuts)]
     blocks = [
         [turn(piece, "dp", by) if by else piece for piece in own_w] for by in range(replicas)

time: 577 us -> 568 us (0.984)
  waiting for transfers between devices: 381 us -> 373 us
    ppermute x16, waiting for transfers between devices: 188 us -> 181 us  [hop(): return lax.ppermute(value, 'section', pairs)]
  transfers between devices with their start and end apart: 46 -> 43, of which waited for: 11 -> 11; matrix products, arithmetic and copies ran while one was open for 1% -> 1% of each run, Pallas kernels for 12% -> 12%
where the time goes in v4:
time: 568 us; the launch traced here: 559 us
  waiting for transfers between devices  373 us (66%)
  Pallas kernels  89.4 us (16%)
  starting transfers between devices  46.7 us (8%)
  between operations  17.6 us (3%)
  blocking collectives  17.2 us (3%)
  local copies, waits for them, and re-layouts  12.2 us (2%)
    ppermute x16, waiting for transfers between devices, hop(): return lax.ppermute(value, 'section', pairs)  181 us
    all_to_all x3, waiting for transfers between devices, relocate(): lax.all_to_all(pieces, 'section', split_axis=0, concat_axis=2, tiled=True)  114 us
    ppermute x13, waiting for transfers between devices, turn(): lax.ppermute(value, axis, [(i, (i + by) % count) for i in range(count)])  74.5 us
    pallas_call x9, Pallas kernels, forward_step(): pl.pallas_call(body, in_specs=[SCALAR, WHOLE, WHOLE, WHOLE], out_specs=[W...  20.7 us
    ppermute x16, starting transfers between devices, hop(): return lax.ppermute(value, 'section', pairs)  20.3 us
    pallas_call x1, Pallas kernels, adam(): pl.pallas_call(body, grid_spec=pltpu.PrefetchScalarGridSpec(num_scalar_pr...  18.8 us
    all_to_all x3, starting transfers between devices, relocate(): lax.all_to_all(pieces, 'section', split_axis=0, concat_axis=2, tiled=True)  17.4 us
    all_gather x8, blocking collectives, forward_tick(): arriving = lax.all_gather(hop(output, tick, 1), 'mp', axis=1, tiled=True)  17.2 us
  transfers between devices with their start and end apart: 43, of which 11 were waited for; matrix products, arithmetic and copies ran while one was open for 1% of the time, Pallas kernels for 12%

profile of v4, /device:TPU:0, one launch (start us, length us, event | category | flops | bytes accessed | tf_op | source)
XLA Modules:
  0.0 559.4 jit_solution(9928326046716250371)
XLA Ops:
  8.7 4.5 shard_map.94
  14.2 4.1 copy-done
  18.4 4.4 shard_map.95
  22.8 7.3 %all-to-all-start = ((bf16[8,1,1,208,896]{4,3,2,1,0:T(8,128)(2,1)}), bf16[8,1,1,208,896]{4,3,2,1,0:T(8,128)(2,1)S(1)}, u32[]{:S(2)}, u32[]{:S(2)}) async-start(bf16[8,1,1,208,896]{4,3,2,1,0:T(8,128)(2,1)} %get-tuple-element.146), calls=%async_computation | async-start | bytes 5963776 | tf_op jit(solution)/shard_map/all_to_all | solution.py:35
  31.6 65.8 %all-to-all-done = bf16[8,1,1,208,896]{4,3,2,1,0:T(8,128)(2,1)S(1)} async-done(((bf16[8,1,1,208,896]{4,3,2,1,0:T(8,128)(2,1)}), bf16[8,1,1,208,896]{4,3,2,1,0:T(8,128)(2,1)S(1)}, u32[]{:S(2)}, u32[]{:S(2)}) %all-to-all-start) | async-done | bytes 2981920 | tf_op jit(solution)/shard_map/all_to_all | solution.py:35
  97.4 4.4 all-to-all-start.2
  103.1 4.6 shard_map.123
  110.6 62.7 %collective-permute-done.refs_3_ = bf16[1664,896]{1,0:T(8,128)(2,1)} collective-permute-done((bf16[1664,896]{1,0:T(8,128)(2,1)S(1)}, bf16[1664,896]{1,0:T(8,128)(2,1)}, u32[]{:S(2)}, u32[]{:S(2)}) %collective-permute-start) | collective-permute-done | bytes 2981920 | tf_op jit(solution)/shard_map/ppermute | solution.py:26
  175.2 3.6 shard_map.96
  178.8 5.7 %all-to-all-start.1 = ((bf16[8,1,1,208,768]{4,3,2,1,0:T(8,128)(2,1)}), bf16[8,1,1,208,768]{4,3,2,1,0:T(8,128)(2,1)}, u32[]{:S(2)}, u32[]{:S(2)}) async-start(bf16[8,1,1,208,768]{4,3,2,1,0:T(8,128)(2,1)} %get-tuple-element.147), calls=%async_computation.1 | async-start | bytes 5111808 | tf_op jit(solution)/shard_map/all_to_all | solution.py:35
  188.6 48.0 %all-to-all-done.1 = bf16[8,1,1,208,768]{4,3,2,1,0:T(8,128)(2,1)} async-done(((bf16[8,1,1,208,768]{4,3,2,1,0:T(8,128)(2,1)}), bf16[8,1,1,208,768]{4,3,2,1,0:T(8,128)(2,1)}, u32[]{:S(2)}, u32[]{:S(2)}) %all-to-all-start.1) | async-done | bytes 2555936 | tf_op jit(solution)/shard_map/all_to_all | solution.py:35
  238.4 2.5 collective-permute-done.1.refs_2_
  240.9 4.3 shard_map.97.w_ref
  245.2 2.2 shard_map.98
  247.4 5.0 collective-permute-start.2
  253.0 2.8 collective-permute-done.2
  258.0 2.2 shard_map.99
  260.2 4.4 collective-permute-start.3
  264.9 4.5 collective-permute-done.3
  271.5 2.2 shard_map.100
  280.1 2.3 all_gather.93.x_ref
  282.4 2.2 shard_map.102
  287.6 2.2 shard_map.103
  292.9 2.2 shard_map.104
  298.2 2.2 shard_map.105
  301.5 2.3 all_gather.97.x_ref
  307.4 2.9 shard_map.108
  343.2 143.8 %collective-permute-done.24.up_ref = bf16[64,1664]{1,0:T(8,128)(2,1)S(1)} collective-permute-done((bf16[64,1664]{1,0:T(8,128)(2,1)S(1)}, bf16[64,1664]{1,0:T(8,128)(2,1)S(1)}, u32[]{:S(2)}, u32[]{:S(2)}) %collective-permute-start.24) | collective-permute-done | bytes 213024 | tf_op jit(solution)/shard_map/ppermute | solution.py:476
  492.0 29.4 %collective-permute-done.26 = bf16[64,1664]{1,0:T(8,128)(2,1)S(1)} collective-permute-done((bf16[64,1664]{1,0:T(8,128)(2,1)S(1)}, bf16[64,1664]{1,0:T(8,128)(2,1)S(1)}, u32[]{:S(2)}, u32[]{:S(2)}) %collective-permute-start.26) | collective-permute-done | bytes 213024 | tf_op jit(solution)/shard_map/ppermute | solution.py:476
  524.3 5.4 collective-permute-done.28
  529.7 3.5 collective-permute-done.27
  533.6 18.8 %shard_map.124 = (f32[8,208,1664]{2,1,0:T(8,128)}, bf16[8,208,1664]{2,1,0:T(8,128)(2,1)}, bf16[8,208,1664]{2,1,0:T(8,128)(2,1)}) custom-call(s32[8]{0:T(128)S(1)} %iota_xor_fusion.order_ref, s32[8]{0:T(128)S(1)} %compare_convert_fusion.side_ref, bf16[8,208,256]{2,1,0:T(8,128)(2,1)S(1)} %bitcast.221, bf16[256,1664]{1,0:T(8,128)(2,1)S(1)} %pad_maximum_fusion.dpre_ref, ...), custom_call_target="tpu_custom_call" | custom-call | tf_op jit(solution)/shard_map/pallas_call | solution.py:369
  (203 shorter events, 79.1 us)
Async XLA Ops:
  7.2 526.1 %all-gather.23.cloned.1.call-start = ((), (), s32[]{:S(2)}) async-start(), calls=%async_computation.3 | async-start | bytes 3194880 | tf_op jit(solution)/shard_map/all_gather | solution.py:440
  22.8 74.6 %all-to-all-start = ((bf16[8,1,1,208,896]{4,3,2,1,0:T(8,128)(2,1)}), bf16[8,1,1,208,896]{4,3,2,1,0:T(8,128)(2,1)S(1)}, u32[]{:S(2)}, u32[]{:S(2)}) async-start(bf16[8,1,1,208,896]{4,3,2,1,0:T(8,128)(2,1)} %get-tuple-element.146), calls=%async_computation | async-start | bytes 5963776 | tf_op jit(solution)/shard_map/all_to_all | solution.py:35
  30.1 503.2 %all-gather.25.cloned.1.call-start = ((), (), s32[]{:S(2)}) async-start(), calls=%async_computation.4 | async-start | bytes 3194880 | tf_op jit(solution)/shard_map/all_gather | solution.py:440
  30.8 502.5 %all-gather.27.cloned.1.call-start = ((), (), s32[]{:S(2)}) async-start(), calls=%async_computation.5 | async-start | bytes 3194880 | tf_op jit(solution)/shard_map/all_gather | solution.py:440
  97.4 81.4 %all-to-all-start.2 = ((bf16[8,1,1,208,768]{4,3,2,1,0:T(8,128)(2,1)}), bf16[8,1,1,208,768]{4,3,2,1,0:T(8,128)(2,1)}, u32[]{:S(2)}, u32[]{:S(2)}) async-start(bf16[8,1,1,208,768]{4,3,2,1,0:T(8,128)(2,1)} %get-tuple-element.148), calls=%async_computation.2 | async-start | bytes 5111808 | tf_op jit(solution)/shard_map/all_to_all | solution.py:35
  101.8 431.6 %all-gather.29.cloned.1.call-start = ((), (), s32[]{:S(2)}) async-start(), calls=%async_computation.6 | async-start | bytes 1597440 | tf_op jit(solution)/shard_map/all_gather | solution.py:440
  107.7 425.7 %all-gather.31.cloned.1.call-start = ((), (), s32[]{:S(2)}) async-start(), calls=%async_computation.7 | async-start | bytes 1597440 | tf_op jit(solution)/shard_map/all_gather | solution.py:440
  107.7 65.6 %collective-permute-start = (bf16[1664,896]{1,0:T(8,128)(2,1)S(1)}, bf16[1664,896]{1,0:T(8,128)(2,1)}, u32[]{:S(2)}, u32[]{:S(2)}) collective-permute-start(bf16[1664,896]{1,0:T(8,128)(2,1)S(1)} %bitcast.224), channel_id=1, source_target_pairs={{0,2},{2,0},{1,3},{3,1},{4,6},{6,4},{5,7},{7,5},{8,10},{10,8},{9,1... | collective-permute-start | bytes 8945672 | tf_op jit(solution)/shard_map/ppermute | solution.py:26
  109.3 424.1 %all-gather.33.cloned.1.call-start = ((), (), s32[]{:S(2)}) async-start(), calls=%async_computation.8 | async-start | bytes 1597440 | tf_op jit(solution)/shard_map/all_gather | solution.py:440
  109.9 423.6 %all-gather.35.cloned.1.call-start = ((), (), s32[]{:S(2)}) async-start(), calls=%async_computation.9 | async-start | bytes 1597440 | tf_op jit(solution)/shard_map/all_gather | solution.py:440
  178.8 57.8 %all-to-all-start.1 = ((bf16[8,1,1,208,768]{4,3,2,1,0:T(8,128)(2,1)}), bf16[8,1,1,208,768]{4,3,2,1,0:T(8,128)(2,1)}, u32[]{:S(2)}, u32[]{:S(2)}) async-start(bf16[8,1,1,208,768]{4,3,2,1,0:T(8,128)(2,1)} %get-tuple-element.147), calls=%async_computation.1 | async-start | bytes 5111808 | tf_op jit(solution)/shard_map/all_to_all | solution.py:35
  184.5 349.0 %all-gather.37.cloned.1.call-start = ((), (), s32[]{:S(2)}) async-start(), calls=%async_computation.10 | async-start | bytes 1597440 | tf_op jit(solution)/shard_map/all_gather | solution.py:440
  185.3 348.2 %all-gather.39.cloned.1.call-start = ((), (), s32[]{:S(2)}) async-start(), calls=%async_computation.11 | async-start | bytes 1597440 | tf_op jit(solution)/shard_map/all_gather | solution.py:440
  185.6 55.3 %collective-permute-start.1 = (bf16[1664,768]{1,0:T(8,128)(2,1)}, bf16[1664,768]{1,0:T(8,128)(2,1)}, u32[]{:S(2)}, u32[]{:S(2)}) collective-permute-start(bf16[1664,768]{1,0:T(8,128)(2,1)} %bitcast.8.refs_0_), channel_id=1, source_target_pairs={{0,2},{2,0},{1,3},{3,1},{4,6},{6,4},{5,7},{7,5},{8,10},{10,8},{9,1... | collective-permute-start | bytes 7667720 | tf_op jit(solution)/shard_map/ppermute | solution.py:26
  187.2 346.4 %all-gather.41.cloned.1.call-start = ((), (), s32[]{:S(2)}) async-start(), calls=%async_computation.12 | async-start | bytes 1597440 | tf_op jit(solution)/shard_map/all_gather | solution.py:440
  187.8 345.8 %all-gather.43.cloned.1.call-start = ((), (), s32[]{:S(2)}) async-start(), calls=%async_computation.13 | async-start | bytes 1597440 | tf_op jit(solution)/shard_map/all_gather | solution.py:440
  247.4 8.3 %collective-permute-start.2 = (bf16[64,1664]{1,0:T(8,128)(2,1)S(1)}, bf16[64,1664]{1,0:T(8,128)(2,1)S(1)}, u32[]{:S(2)}, u32[]{:S(2)}) collective-permute-start(bf16[64,1664]{1,0:T(8,128)(2,1)S(1)} %get-tuple-element.150), channel_id=1, source_target_pairs={{0,4},{1,5},{2,6},{3,7}} | collective-permute-start | bytes 638984 | tf_op jit(solution)/shard_map/ppermute | solution.py:476
  260.2 9.2 %collective-permute-start.3 = (bf16[64,1664]{1,0:T(8,128)(2,1)S(1)}, bf16[64,1664]{1,0:T(8,128)(2,1)S(1)}, u32[]{:S(2)}, u32[]{:S(2)}) collective-permute-start(bf16[64,1664]{1,0:T(8,128)(2,1)S(1)} %get-tuple-element.153), channel_id=1, source_target_pairs={{4,8},{0,4},{5,9},{1,5},{6,10},{2,6},{7,11},{3,7}} | collective-permute-start | bytes 638984 | tf_op jit(solution)/shard_map/ppermute | solution.py:476
  310.3 1.5 collective-permute-start.11
  314.4 2.0 collective-permute-start.13
  319.0 2.2 collective-permute-start.15
  323.9 2.1 collective-permute-start.17
  326.0 2.6 collective-permute-start.18
  327.0 196.6 %collective-permute-start.10 = (bf16[128,1664]{1,0:T(8,128)(2,1)S(1)}, bf16[128,1664]{1,0:T(8,128)(2,1)S(1)}, u32[]{:S(2)}, u32[]{:S(2)}) collective-permute-start(bf16[128,1664]{1,0:T(8,128)(2,1)S(1)} %get-tuple-element.314), channel_id=1, source_target_pairs={{0,2},{2,0},{1,3},{3,1},{4,6},{6,4},{5,7},{7,5},{8,10},{10,8},{9,1... | collective-permute-start | bytes 1277960 | tf_op jit(solution)/shard_map/ppermute | solution.py:26
  330.4 2.0 collective-permute-start.19
  335.0 2.3 collective-permute-start.21
  339.9 1.9 collective-permute-start.23
  341.8 145.1 %collective-permute-start.24 = (bf16[64,1664]{1,0:T(8,128)(2,1)S(1)}, bf16[64,1664]{1,0:T(8,128)(2,1)S(1)}, u32[]{:S(2)}, u32[]{:S(2)}) collective-permute-start(bf16[64,1664]{1,0:T(8,128)(2,1)S(1)} %add_convert_fusion.1), channel_id=1, source_target_pairs={{4,0},{8,4},{5,1},{9,5},{6,2},{10,6},{7,3},{11,7}} | collective-permute-start | bytes 638984 | tf_op jit(solution)/shard_map/ppermute | solution.py:476
  488.7 1.9 collective-permute-start.25
  490.7 30.8 %collective-permute-start.26 = (bf16[64,1664]{1,0:T(8,128)(2,1)S(1)}, bf16[64,1664]{1,0:T(8,128)(2,1)S(1)}, u32[]{:S(2)}, u32[]{:S(2)}) collective-permute-start(bf16[64,1664]{1,0:T(8,128)(2,1)S(1)} %add_convert_fusion), channel_id=1, source_target_pairs={{4,0},{5,1},{6,2},{7,3}} | collective-permute-start | bytes 638984 | tf_op jit(solution)/shard_map/ppermute | solution.py:476
  521.5 8.2 %collective-permute-start.28 = (bf16[64,1664]{1,0:T(8,128)(2,1)S(1)}, bf16[64,1664]{1,0:T(8,128)(2,1)S(1)}, u32[]{:S(2)}, u32[]{:S(2)}) collective-permute-start(bf16[64,1664]{1,0:T(8,128)(2,1)S(1)} %slice_bitcast_fusion), channel_id=1, source_target_pairs={{0,2},{2,0},{1,3},{3,1},{4,6},{6,4},{5,7},{7,5},{8,10},{10,8},{9,1... | collective-permute-start | bytes 638984 | tf_op jit(solution)/shard_map/ppermute | solution.py:26
  523.0 10.2 %collective-permute-start.27 = (bf16[64,1664]{1,0:T(8,128)(2,1)S(1)}, bf16[64,1664]{1,0:T(8,128)(2,1)S(1)}, u32[]{:S(2)}, u32[]{:S(2)}) collective-permute-start(bf16[64,1664]{1,0:T(8,128)(2,1)S(1)} %get-tuple-element.317), channel_id=1, source_target_pairs={{0,2},{2,0},{1,3},{3,1},{4,6},{6,4},{5,7},{7,5},{8,10},{10,8},{9,1... | collective-permute-start | bytes 638984 | tf_op jit(solution)/shard_map/ppermute | solution.py:26
  (17 other events, 33.0 us)
Sparse Core Ops, SparseCore 0:
  14.3 68.1 all-gather.22
  84.1 77.3 all-gather.24
  163.0 59.4 all-gather.26
  223.9 44.3 all-gather.28
  269.7 31.0 all-gather.30
  302.2 38.2 all-gather.32
  342.1 33.6 all-gather.34
  377.4 21.6 all-gather.36
  400.6 35.7 all-gather.38
  437.8 32.7 all-gather.40
  472.1 34.4 all-gather.42

commit v5 on v4

--- a/solution.py
+++ b/solution.py
@@ -445,7 +445,11 @@
     moment_one = relocate(ordered_m)
     later = picks[early:] + zero_after(own_w[-1])
     _, sent = picked(later, inverse, travelling, edges, False)
-    moments += [[meet(piece, by) for piece in sent[by - early]] for by in range(early, sections)]
+    crossing = {
+        by: [meet(piece, by) for piece in sent[by - early]]
+        for by in sorted(range(early, sections), key=lambda by: (1 - by % 2, by))
+    }
+    moments += [crossing[by] for by in range(early, sections)]
     entry_section = section_index
     weight = resident((replica_index + zero_after(moment_one)).reshape(1), blocks, cuts)
 

time: 568 us -> 568 us (level)
  no operation moved by 1% of the time
where the time goes in v5:
time: 568 us; the launch traced here: 559 us
  waiting for transfers between devices  373 us (66%)
  Pallas kernels  89.4 us (16%)
  starting transfers between devices  46.7 us (8%)
  between operations  17.6 us (3%)
  blocking collectives  17.2 us (3%)
  local copies, waits for them, and re-layouts  12.2 us (2%)
    ppermute x16, waiting for transfers between devices, hop(): return lax.ppermute(value, 'section', pairs)  181 us
    all_to_all x3, waiting for transfers between devices, relocate(): lax.all_to_all(pieces, 'section', split_axis=0, concat_axis=2, tiled=True)  114 us
    ppermute x13, waiting for transfers between devices, turn(): lax.ppermute(value, axis, [(i, (i + by) % count) for i in range(count)])  74.5 us
    pallas_call x9, Pallas kernels, forward_step(): pl.pallas_call(body, in_specs=[SCALAR, WHOLE, WHOLE, WHOLE], out_specs=[W...  20.7 us
    ppermute x16, starting transfers between devices, hop(): return lax.ppermute(value, 'section', pairs)  20.3 us
    pallas_call x1, Pallas kernels, adam(): pl.pallas_call(body, grid_spec=pltpu.PrefetchScalarGridSpec(num_scalar_pr...  18.8 us
    all_to_all x3, starting transfers between devices, relocate(): lax.all_to_all(pieces, 'section', split_axis=0, concat_axis=2, tiled=True)  17.4 us
    all_gather x8, blocking collectives, forward_tick(): arriving = lax.all_gather(hop(output, tick, 1), 'mp', axis=1, tiled=True)  17.2 us
  transfers between devices with their start and end apart: 43, of which 11 were waited for; matrix products, arithmetic and copies ran while one was open for 1% of the time, Pallas kernels for 12%

profile of v5, /device:TPU:0, one launch (start us, length us, event | category | flops | bytes accessed | tf_op | source)
XLA Modules:
  0.0 559.4 jit_solution(9928326046716250371)
XLA Ops:
  8.7 4.5 shard_map.94
  14.2 4.1 copy-done
  18.4 4.4 shard_map.95
  22.8 7.3 %all-to-all-start = ((bf16[8,1,1,208,896]{4,3,2,1,0:T(8,128)(2,1)}), bf16[8,1,1,208,896]{4,3,2,1,0:T(8,128)(2,1)S(1)}, u32[]{:S(2)}, u32[]{:S(2)}) async-start(bf16[8,1,1,208,896]{4,3,2,1,0:T(8,128)(2,1)} %get-tuple-element.146), calls=%async_computation | async-start | bytes 5963776 | tf_op jit(solution)/shard_map/all_to_all | solution.py:35
  31.6 65.8 %all-to-all-done = bf16[8,1,1,208,896]{4,3,2,1,0:T(8,128)(2,1)S(1)} async-done(((bf16[8,1,1,208,896]{4,3,2,1,0:T(8,128)(2,1)}), bf16[8,1,1,208,896]{4,3,2,1,0:T(8,128)(2,1)S(1)}, u32[]{:S(2)}, u32[]{:S(2)}) %all-to-all-start) | async-done | bytes 2981920 | tf_op jit(solution)/shard_map/all_to_all | solution.py:35
  97.4 4.4 all-to-all-start.2
  103.1 4.6 shard_map.123
  110.6 62.7 %collective-permute-done.refs_3_ = bf16[1664,896]{1,0:T(8,128)(2,1)} collective-permute-done((bf16[1664,896]{1,0:T(8,128)(2,1)S(1)}, bf16[1664,896]{1,0:T(8,128)(2,1)}, u32[]{:S(2)}, u32[]{:S(2)}) %collective-permute-start) | collective-permute-done | bytes 2981920 | tf_op jit(solution)/shard_map/ppermute | solution.py:26
  175.2 3.6 shard_map.96
  178.8 5.7 %all-to-all-start.1 = ((bf16[8,1,1,208,768]{4,3,2,1,0:T(8,128)(2,1)}), bf16[8,1,1,208,768]{4,3,2,1,0:T(8,128)(2,1)}, u32[]{:S(2)}, u32[]{:S(2)}) async-start(bf16[8,1,1,208,768]{4,3,2,1,0:T(8,128)(2,1)} %get-tuple-element.147), calls=%async_computation.1 | async-start | bytes 5111808 | tf_op jit(solution)/shard_map/all_to_all | solution.py:35
  188.6 48.0 %all-to-all-done.1 = bf16[8,1,1,208,768]{4,3,2,1,0:T(8,128)(2,1)} async-done(((bf16[8,1,1,208,768]{4,3,2,1,0:T(8,128)(2,1)}), bf16[8,1,1,208,768]{4,3,2,1,0:T(8,128)(2,1)}, u32[]{:S(2)}, u32[]{:S(2)}) %all-to-all-start.1) | async-done | bytes 2555936 | tf_op jit(solution)/shard_map/all_to_all | solution.py:35
  238.4 2.5 collective-permute-done.1.refs_2_
  240.9 4.3 shard_map.97.w_ref
  245.2 2.2 shard_map.98
  247.4 5.0 collective-permute-start.2
  253.0 2.8 collective-permute-done.2
  258.0 2.2 shard_map.99
  260.2 4.4 collective-permute-start.3
  264.9 4.5 collective-permute-done.3
  271.5 2.2 shard_map.100
  280.1 2.3 all_gather.93.x_ref
  282.4 2.2 shard_map.102
  287.6 2.2 shard_map.103
  292.9 2.2 shard_map.104
  298.2 2.2 shard_map.105
  301.5 2.3 all_gather.97.x_ref
  307.4 2.9 shard_map.108
  343.2 143.8 %collective-permute-done.24.up_ref = bf16[64,1664]{1,0:T(8,128)(2,1)S(1)} collective-permute-done((bf16[64,1664]{1,0:T(8,128)(2,1)S(1)}, bf16[64,1664]{1,0:T(8,128)(2,1)S(1)}, u32[]{:S(2)}, u32[]{:S(2)}) %collective-permute-start.24) | collective-permute-done | bytes 213024 | tf_op jit(solution)/shard_map/ppermute | solution.py:480
  492.0 29.4 %collective-permute-done.26 = bf16[64,1664]{1,0:T(8,128)(2,1)S(1)} collective-permute-done((bf16[64,1664]{1,0:T(8,128)(2,1)S(1)}, bf16[64,1664]{1,0:T(8,128)(2,1)S(1)}, u32[]{:S(2)}, u32[]{:S(2)}) %collective-permute-start.26) | collective-permute-done | bytes 213024 | tf_op jit(solution)/shard_map/ppermute | solution.py:480
  524.3 5.4 collective-permute-done.28
  529.7 3.5 collective-permute-done.27
  533.6 18.8 %shard_map.124 = (f32[8,208,1664]{2,1,0:T(8,128)}, bf16[8,208,1664]{2,1,0:T(8,128)(2,1)}, bf16[8,208,1664]{2,1,0:T(8,128)(2,1)}) custom-call(s32[8]{0:T(128)S(1)} %iota_xor_fusion.order_ref, s32[8]{0:T(128)S(1)} %compare_convert_fusion.side_ref, bf16[8,208,256]{2,1,0:T(8,128)(2,1)S(1)} %bitcast.221, bf16[256,1664]{1,0:T(8,128)(2,1)S(1)} %pad_maximum_fusion.dpre_ref, ...), custom_call_target="tpu_custom_call" | custom-call | tf_op jit(solution)/shard_map/pallas_call | solution.py:369
  (203 shorter events, 79.1 us)
Async XLA Ops:
  7.2 526.1 %all-gather.23.cloned.1.call-start = ((), (), s32[]{:S(2)}) async-start(), calls=%async_computation.3 | async-start | bytes 3194880 | tf_op jit(solution)/shard_map/all_gather | solution.py:440
  22.8 74.6 %all-to-all-start = ((bf16[8,1,1,208,896]{4,3,2,1,0:T(8,128)(2,1)}), bf16[8,1,1,208,896]{4,3,2,1,0:T(8,128)(2,1)S(1)}, u32[]{:S(2)}, u32[]{:S(2)}) async-start(bf16[8,1,1,208,896]{4,3,2,1,0:T(8,128)(2,1)} %get-tuple-element.146), calls=%async_computation | async-start | bytes 5963776 | tf_op jit(solution)/shard_map/all_to_all | solution.py:35
  30.1 503.2 %all-gather.25.cloned.1.call-start = ((), (), s32[]{:S(2)}) async-start(), calls=%async_computation.4 | async-start | bytes 3194880 | tf_op jit(solution)/shard_map/all_gather | solution.py:440
  30.8 502.5 %all-gather.27.cloned.1.call-start = ((), (), s32[]{:S(2)}) async-start(), calls=%async_computation.5 | async-start | bytes 3194880 | tf_op jit(solution)/shard_map/all_gather | solution.py:440
  97.4 81.4 %all-to-all-start.2 = ((bf16[8,1,1,208,768]{4,3,2,1,0:T(8,128)(2,1)}), bf16[8,1,1,208,768]{4,3,2,1,0:T(8,128)(2,1)}, u32[]{:S(2)}, u32[]{:S(2)}) async-start(bf16[8,1,1,208,768]{4,3,2,1,0:T(8,128)(2,1)} %get-tuple-element.148), calls=%async_computation.2 | async-start | bytes 5111808 | tf_op jit(solution)/shard_map/all_to_all | solution.py:35
  101.8 431.6 %all-gather.29.cloned.1.call-start = ((), (), s32[]{:S(2)}) async-start(), calls=%async_computation.6 | async-start | bytes 1597440 | tf_op jit(solution)/shard_map/all_gather | solution.py:440
  107.7 425.7 %all-gather.31.cloned.1.call-start = ((), (), s32[]{:S(2)}) async-start(), calls=%async_computation.7 | async-start | bytes 1597440 | tf_op jit(solution)/shard_map/all_gather | solution.py:440
  107.7 65.6 %collective-permute-start = (bf16[1664,896]{1,0:T(8,128)(2,1)S(1)}, bf16[1664,896]{1,0:T(8,128)(2,1)}, u32[]{:S(2)}, u32[]{:S(2)}) collective-permute-start(bf16[1664,896]{1,0:T(8,128)(2,1)S(1)} %bitcast.224), channel_id=1, source_target_pairs={{0,2},{2,0},{1,3},{3,1},{4,6},{6,4},{5,7},{7,5},{8,10},{10,8},{9,1... | collective-permute-start | bytes 8945672 | tf_op jit(solution)/shard_map/ppermute | solution.py:26
  109.3 424.1 %all-gather.33.cloned.1.call-start = ((), (), s32[]{:S(2)}) async-start(), calls=%async_computation.8 | async-start | bytes 1597440 | tf_op jit(solution)/shard_map/all_gather | solution.py:440
  109.9 423.6 %all-gather.35.cloned.1.call-start = ((), (), s32[]{:S(2)}) async-start(), calls=%async_computation.9 | async-start | bytes 1597440 | tf_op jit(solution)/shard_map/all_gather | solution.py:440
  178.8 57.8 %all-to-all-start.1 = ((bf16[8,1,1,208,768]{4,3,2,1,0:T(8,128)(2,1)}), bf16[8,1,1,208,768]{4,3,2,1,0:T(8,128)(2,1)}, u32[]{:S(2)}, u32[]{:S(2)}) async-start(bf16[8,1,1,208,768]{4,3,2,1,0:T(8,128)(2,1)} %get-tuple-element.147), calls=%async_computation.1 | async-start | bytes 5111808 | tf_op jit(solution)/shard_map/all_to_all | solution.py:35
  184.5 349.0 %all-gather.37.cloned.1.call-start = ((), (), s32[]{:S(2)}) async-start(), calls=%async_computation.10 | async-start | bytes 1597440 | tf_op jit(solution)/shard_map/all_gather | solution.py:440
  185.3 348.2 %all-gather.39.cloned.1.call-start = ((), (), s32[]{:S(2)}) async-start(), calls=%async_computation.11 | async-start | bytes 1597440 | tf_op jit(solution)/shard_map/all_gather | solution.py:440
  185.6 55.3 %collective-permute-start.1 = (bf16[1664,768]{1,0:T(8,128)(2,1)}, bf16[1664,768]{1,0:T(8,128)(2,1)}, u32[]{:S(2)}, u32[]{:S(2)}) collective-permute-start(bf16[1664,768]{1,0:T(8,128)(2,1)} %bitcast.8.refs_0_), channel_id=1, source_target_pairs={{0,2},{2,0},{1,3},{3,1},{4,6},{6,4},{5,7},{7,5},{8,10},{10,8},{9,1... | collective-permute-start | bytes 7667720 | tf_op jit(solution)/shard_map/ppermute | solution.py:26
  187.2 346.4 %all-gather.41.cloned.1.call-start = ((), (), s32[]{:S(2)}) async-start(), calls=%async_computation.12 | async-start | bytes 1597440 | tf_op jit(solution)/shard_map/all_gather | solution.py:440
  187.8 345.8 %all-gather.43.cloned.1.call-start = ((), (), s32[]{:S(2)}) async-start(), calls=%async_computation.13 | async-start | bytes 1597440 | tf_op jit(solution)/shard_map/all_gather | solution.py:440
  247.4 8.3 %collective-permute-start.2 = (bf16[64,1664]{1,0:T(8,128)(2,1)S(1)}, bf16[64,1664]{1,0:T(8,128)(2,1)S(1)}, u32[]{:S(2)}, u32[]{:S(2)}) collective-permute-start(bf16[64,1664]{1,0:T(8,128)(2,1)S(1)} %get-tuple-element.150), channel_id=1, source_target_pairs={{0,4},{1,5},{2,6},{3,7}} | collective-permute-start | bytes 638984 | tf_op jit(solution)/shard_map/ppermute | solution.py:480
  260.2 9.2 %collective-permute-start.3 = (bf16[64,1664]{1,0:T(8,128)(2,1)S(1)}, bf16[64,1664]{1,0:T(8,128)(2,1)S(1)}, u32[]{:S(2)}, u32[]{:S(2)}) collective-permute-start(bf16[64,1664]{1,0:T(8,128)(2,1)S(1)} %get-tuple-element.153), channel_id=1, source_target_pairs={{4,8},{0,4},{5,9},{1,5},{6,10},{2,6},{7,11},{3,7}} | collective-permute-start | bytes 638984 | tf_op jit(solution)/shard_map/ppermute | solution.py:480
  310.3 1.5 collective-permute-start.11
  314.4 2.0 collective-permute-start.13
  319.0 2.2 collective-permute-start.15
  323.9 2.1 collective-permute-start.17
  326.0 2.6 collective-permute-start.18
  327.0 196.6 %collective-permute-start.10 = (bf16[128,1664]{1,0:T(8,128)(2,1)S(1)}, bf16[128,1664]{1,0:T(8,128)(2,1)S(1)}, u32[]{:S(2)}, u32[]{:S(2)}) collective-permute-start(bf16[128,1664]{1,0:T(8,128)(2,1)S(1)} %get-tuple-element.314), channel_id=1, source_target_pairs={{0,2},{2,0},{1,3},{3,1},{4,6},{6,4},{5,7},{7,5},{8,10},{10,8},{9,1... | collective-permute-start | bytes 1277960 | tf_op jit(solution)/shard_map/ppermute | solution.py:26
  330.4 2.0 collective-permute-start.19
  335.0 2.3 collective-permute-start.21
  339.9 1.9 collective-permute-start.23
  341.8 145.1 %collective-permute-start.24 = (bf16[64,1664]{1,0:T(8,128)(2,1)S(1)}, bf16[64,1664]{1,0:T(8,128)(2,1)S(1)}, u32[]{:S(2)}, u32[]{:S(2)}) collective-permute-start(bf16[64,1664]{1,0:T(8,128)(2,1)S(1)} %add_convert_fusion.1), channel_id=1, source_target_pairs={{4,0},{8,4},{5,1},{9,5},{6,2},{10,6},{7,3},{11,7}} | collective-permute-start | bytes 638984 | tf_op jit(solution)/shard_map/ppermute | solution.py:480
  488.7 1.9 collective-permute-start.25
  490.7 30.8 %collective-permute-start.26 = (bf16[64,1664]{1,0:T(8,128)(2,1)S(1)}, bf16[64,1664]{1,0:T(8,128)(2,1)S(1)}, u32[]{:S(2)}, u32[]{:S(2)}) collective-permute-start(bf16[64,1664]{1,0:T(8,128)(2,1)S(1)} %add_convert_fusion), channel_id=1, source_target_pairs={{4,0},{5,1},{6,2},{7,3}} | collective-permute-start | bytes 638984 | tf_op jit(solution)/shard_map/ppermute | solution.py:480
  521.5 8.2 %collective-permute-start.28 = (bf16[64,1664]{1,0:T(8,128)(2,1)S(1)}, bf16[64,1664]{1,0:T(8,128)(2,1)S(1)}, u32[]{:S(2)}, u32[]{:S(2)}) collective-permute-start(bf16[64,1664]{1,0:T(8,128)(2,1)S(1)} %slice_bitcast_fusion), channel_id=1, source_target_pairs={{0,2},{2,0},{1,3},{3,1},{4,6},{6,4},{5,7},{7,5},{8,10},{10,8},{9,1... | collective-permute-start | bytes 638984 | tf_op jit(solution)/shard_map/ppermute | solution.py:26
  523.0 10.2 %collective-permute-start.27 = (bf16[64,1664]{1,0:T(8,128)(2,1)S(1)}, bf16[64,1664]{1,0:T(8,128)(2,1)S(1)}, u32[]{:S(2)}, u32[]{:S(2)}) collective-permute-start(bf16[64,1664]{1,0:T(8,128)(2,1)S(1)} %get-tuple-element.317), channel_id=1, source_target_pairs={{0,2},{2,0},{1,3},{3,1},{4,6},{6,4},{5,7},{7,5},{8,10},{10,8},{9,1... | collective-permute-start | bytes 638984 | tf_op jit(solution)/shard_map/ppermute | solution.py:26
  (17 other events, 33.0 us)
Sparse Core Ops, SparseCore 0:
  14.3 68.1 all-gather.22
  84.1 77.3 all-gather.24
  163.0 59.4 all-gather.26
  223.9 44.3 all-gather.28
  269.7 31.0 all-gather.30
  302.2 38.2 all-gather.32
  342.1 33.6 all-gather.34
  377.4 21.6 all-gather.36
  400.6 35.7 all-gather.38
  437.8 32.7 all-gather.40
  472.1 34.4 all-gather.42
